TPU v7x, 128 devices: a whole 4x4x4 slice. The times are simulated.
128 devices in a mesh: gx: 4 (over x), gy: 4 (over z), gz: 8 (over y, core).
Axes of the slice: x: 4, y: 4, z: 4, core: 2. Of those that a mesh axis runs over, the one named last changes fastest.
Arguments:
- sources: bfloat16 [8, 32, 32, 27, 128], P('gx', 'gy', 'gz'), may hold values from -6 to 6
- geometry: float32 [8, 32, 32, 108], P('gx', 'gy', 'gz'), may hold values from 0.6 to 4.8
- rock_class: int32 [8, 32, 32], P('gx', 'gy', 'gz'), may hold values from 0 to 15
- permeability: float32 [16, 3], replicated, may hold values from 0.1 to 10
- mass_inv: float32 [108, 108], replicated, may hold values from -0.015 to 2.7, as said below
- div_map: float32 [27, 108], replicated, may hold values from -0.625 to 0.625
- trace_map: float32 [54, 108], replicated, may hold values from -0.625 to 0.625
- dirichlet: int32 [8, 32, 32, 3], P('gx', 'gy', 'gz'), may hold values 0 or 1
Outputs:
- traces: float32 [8, 32, 32, 27, 128], P('gx', 'gy', 'gz')
- flux: bfloat16 [8, 32, 32, 108, 128], P('gx', 'gy', 'gz')
Inputs may be any that keep to these rules, and one draw needn't show every extreme that they name: `mass_inv`: symmetric; every diagonal entry exceeds the sum of the magnitudes of the other entries of its row.
All inputs are finite; a program needn't handle non-finite values. No bound on the sum of `dirichlet` on one device may be relied on, other than what follows from the above.
Results may differ from a plain program's by a relative error of at most 0.0029.
Values sent between devices are 32-bit elements; how exact they have to be, the bound alone decides.
A program may use at most 128 MiB of HBM per device.

v0:
```python
import jax
import jax.numpy as jnp
from jax import lax
from jax.sharding import PartitionSpec as P

ITERS = 3


finest = lax.Precision.HIGHEST


def passed_along(value, axis, steps):
    count = lax.axis_size(axis)
    pairs = [(source, (source + steps) % count) for source in range(count)]
    return lax.ppermute(value, axis, pairs)


def solve_small(factor, right):
    middle = lax.linalg.triangular_solve(factor, right, left_side=True, lower=True)
    return lax.linalg.triangular_solve(factor, middle, left_side=True, lower=True, transpose_a=True)


def element_blocks(geometry, rock_class, permeability, mass_inv, div_map, trace_map):
    elements = rock_class.shape[0] * rock_class.shape[1] * rock_class.shape[2]
    classes = permeability.shape[0]
    flux_dofs = mass_inv.shape[0]
    labels = rock_class.reshape(elements)
    onehot = (labels[:, None] == jnp.arange(classes, dtype=jnp.int32)[None, :]).astype(jnp.float32)
    rooted = jnp.dot(
        onehot, jnp.sqrt(permeability), precision=finest, preferred_element_type=jnp.float32
    )
    scaling = geometry.reshape(elements, flux_dofs) * jnp.repeat(rooted, flux_dofs // 3, axis=1)
    joined = jnp.concatenate([div_map, trace_map], axis=0)
    scaled = joined[None, :, :] * scaling[:, None, :]
    stacked_rows = joined.shape[0]
    applied = jnp.dot(
        scaled.reshape(elements * stacked_rows, flux_dofs),
        mass_inv,
        precision=finest,
        preferred_element_type=jnp.float32,
    )
    applied = applied.reshape(elements, stacked_rows, flux_dofs)
    coupled = jnp.einsum("eaj,ebj->eab", applied, scaled, precision=finest)
    pressures = div_map.shape[0]
    schur = coupled[:, :pressures, :pressures]
    mixed = coupled[:, :pressures, pressures:]
    factor = jnp.linalg.cholesky(schur)
    solved = solve_small(factor, mixed)
    condensed = coupled[:, pressures:, pressures:] - jnp.einsum(
        "ept,eps->ets", mixed, solved, precision=finest
    )
    return (joined, scaling, factor, mixed, solved, condensed)


def element_vector(owned, upper_side):
    elements = owned.shape[0] * owned.shape[1] * owned.shape[2]
    columns = owned.shape[-1]
    return jnp.concatenate(
        [owned.reshape(elements, -1, columns), upper_side.reshape(elements, -1, columns)], axis=1
    )


def split_element(values, block_shape):
    half = values.shape[1] // 2
    columns = values.shape[-1]
    lower_side = values[:, :half].reshape(block_shape + (3, -1, columns))
    upper_side = values[:, half:].reshape(block_shape + (3, -1, columns))
    return (lower_side, upper_side)


def fetch_upper(owned):
    first_x = passed_along(owned[0:1, :, :, 0], "gx", -1)
    first_y = passed_along(owned[:, 0:1, :, 1], "gy", -1)
    first_z = passed_along(owned[:, :, 0:1, 2], "gz", -1)
    upper_x = jnp.concatenate([owned[1:, :, :, 0], first_x], axis=0)
    upper_y = jnp.concatenate([owned[:, 1:, :, 1], first_y], axis=1)
    upper_z = jnp.concatenate([owned[:, :, 1:, 2], first_z], axis=2)
    return jnp.stack([upper_x, upper_y, upper_z], axis=3)


def return_upper(lower_side, upper_side):
    last_x = passed_along(upper_side[-1:, :, :, 0], "gx", 1)
    last_y = passed_along(upper_side[:, -1:, :, 1], "gy", 1)
    last_z = passed_along(upper_side[:, :, -1:, 2], "gz", 1)
    moved_x = jnp.concatenate([last_x, upper_side[:-1, :, :, 0]], axis=0)
    moved_y = jnp.concatenate([last_y, upper_side[:, :-1, :, 1]], axis=1)
    moved_z = jnp.concatenate([last_z, upper_side[:, :, :-1, 2]], axis=2)
    return lower_side + jnp.stack([moved_x, moved_y, moved_z], axis=3)


def combine(first, second, weight):
    return tuple((left + weight * right for left, right in zip(first, second)))


def column_inner(first, second):
    return jnp.sum(first[0] * second[0], axis=(0, 1, 2, 3, 4))


def body(sources, geometry, rock_class, permeability, mass_inv, div_map, trace_map, dirichlet):
    joined, scaling, factor, mixed, solved, condensed = element_blocks(
        geometry, rock_class, permeability, mass_inv, div_map, trace_map
    )
    block_shape = rock_class.shape
    elements = block_shape[0] * block_shape[1] * block_shape[2]
    columns = sources.shape[-1]
    keep = (1 - dirichlet).astype(jnp.float32)[:, :, :, :, None, None]
    forcing = sources.astype(jnp.float32).reshape(elements, -1, columns)
    diag_values = jnp.diagonal(condensed, axis1=1, axis2=2)[:, :, None]

    def assemble(values):
        lower_side, upper_side = split_element(values, block_shape)
        return (return_upper(lower_side, upper_side),)

    def upper_of(vector):
        return fetch_upper(vector[0])

    diag_vector = assemble(diag_values)
    inverse = (keep / diag_vector[0],)

    def masked(vector):
        return (vector[0] * keep,) + tuple(vector[1:])

    def precondition(vector):
        return tuple((scale * item for scale, item in zip(inverse, vector)))

    residual = masked(assemble(jnp.einsum("ept,epr->etr", solved, forcing, precision=finest)))
    solution = tuple((jnp.zeros_like(item) for item in residual))
    precond = precondition(residual)

    def global_sum(local_value):
        return lax.psum(local_value, ("gx", "gy", "gz"))

    direction = precond
    current = global_sum(column_inner(residual, precond))
    for step in range(ITERS):
        operate_values = element_vector(direction[0], upper_of(direction))
        image = masked(
            assemble(jnp.einsum("ets,esr->etr", condensed, operate_values, precision=finest))
        )
        alpha = current / global_sum(column_inner(direction, image))
        solution = combine(solution, direction, alpha)
        residual = combine(residual, image, -alpha)
        precond = precondition(residual)
        following = global_sum(column_inner(residual, precond))
        direction = combine(precond, direction, following / current)
        current = following
    values = element_vector(solution[0], upper_of(solution))
    pressure = -solve_small(
        factor, forcing + jnp.einsum("ept,etr->epr", mixed, values, precision=finest)
    )
    summed = jnp.einsum(
        "ai,ear->eir", joined, jnp.concatenate([pressure, values], axis=1), precision=finest
    )
    flux = -scaling[:, :, None] * jnp.einsum(
        "ij,ejr->eir", mass_inv, scaling[:, :, None] * summed, precision=finest
    )
    traces = solution[0].reshape(block_shape + (-1, columns))
    return (traces, flux.astype(jnp.bfloat16).reshape(block_shape + (-1, columns)))


def solution(mesh):
    placed = (
        P("gx", "gy", "gz", None, None),
        P("gx", "gy", "gz", None),
        P("gx", "gy", "gz"),
        P(),
        P(),
        P(),
        P(),
        P("gx", "gy", "gz", None),
    )
    return jax.shard_map(
        body,
        mesh=mesh,
        in_specs=placed,
        out_specs=(P("gx", "gy", "gz", None, None), P("gx", "gy", "gz", None, None)),
        check_vma=False,
    )
```

profile of v0, /device:TPU:1, one launch (start us, length us, event | category | flops | bytes accessed | tf_op | source)
XLA Modules:
  0.0 682.0 jit_solution(8535642798423830132)
XLA Ops:
  7.2 5.2 fusion
  18.8 160.0 %custom-call.13 = f32[64,27,27]{2,1,0:T(8,128)} custom-call(f32[64,27,27]{2,1,0:T(8,128)} %fusion.44), custom_call_target="Cholesky" | custom-call | tf_op jit(solution)/shard_map/jit(cholesky)/cholesky | solution.py:47
  181.7 9.9 %custom-call.14 = f32[64,1,27,27]{0,2,3,1:T(8,128)S(1)} custom-call(f32[64,1,27,27]{0,3,2,1:T(8,128)} %select_bitcast_fusion), custom_call_target="InvertDiagBlocksLowerTriangular" | custom-call | tf_op jit(solution)/shard_map/triangular_solve | solution.py:20
  210.6 5.8 slice_subtract_fusion
  244.6 2.9 collective-permute-start.8
  250.8 3.2 fusion.13
  260.9 2.9 multiply_reduce_fusion.1
  263.8 65.8 %all-reduce = (f32[128]{0:T(128)}, f32[128]{0:T(128)}) all-reduce(f32[128]{0:T(128)} %get-tuple-element.13, f32[128]{0:T(128)} %get-tuple-element.12), channel_id=1, replica_groups=mesh['gx'=4,'gy'=4,'gz'=8] {'gx','gy','gz'}, use_global_device_ids=true, to_apply=%region_3.4 | all-reduce | flops 256 | bytes 2048 | tf_op jit(solution)/shard_map/psum | solution.py:131
  330.8 3.5 fusion.39
  334.3 64.1 %psum.44 = f32[128]{0:T(128)} all-reduce(f32[128]{0:T(128)} %get-tuple-element.22), channel_id=1, replica_groups=mesh['gx'=4,'gy'=4,'gz'=8] {'gx','gy','gz'}, use_global_device_ids=true, to_apply=%region_7.8 | all-reduce | flops 128 | bytes 1024 | tf_op jit(solution)/shard_map/psum | solution.py:131
  400.9 2.8 multiply_add_fusion.7
  411.9 3.2 fusion.17
  416.8 3.7 collective-permute-done.16
  424.7 65.3 %psum.45 = f32[128]{0:T(128)} all-reduce(f32[128]{0:T(128)} %multiply_reduce_fusion), channel_id=1, replica_groups=mesh['gx'=4,'gy'=4,'gz'=8] {'gx','gy','gz'}, use_global_device_ids=true, to_apply=%region_9.10 | all-reduce | flops 128 | bytes 1024 | tf_op jit(solution)/shard_map/psum | solution.py:131
  491.6 2.9 fusion.40
  494.5 64.0 %psum.46 = f32[128]{0:T(128)} all-reduce(f32[128]{0:T(128)} %fusion.40), channel_id=1, replica_groups=mesh['gx'=4,'gy'=4,'gz'=8] {'gx','gy','gz'}, use_global_device_ids=true, to_apply=%region_11.12 | all-reduce | flops 128 | bytes 1024 | tf_op jit(solution)/shard_map/psum | solution.py:131
  559.2 2.8 multiply_add_fusion
  573.0 3.2 fusion.21
  583.9 66.2 %psum.47 = f32[128]{0:T(128)S(1)} all-reduce(f32[128]{0:T(128)S(1)} %fusion.43), channel_id=1, replica_groups=mesh['gx'=4,'gy'=4,'gz'=8] {'gx','gy','gz'}, use_global_device_ids=true, to_apply=%region_13.14 | all-reduce | flops 128 | bytes 1024 | tf_op jit(solution)/shard_map/psum | solution.py:131
  655.0 3.7 fusion.58
  661.5 2.8 collective-permute-done.26
  665.5 3.5 fusion.36
  671.5 3.7 fusion.7
  675.2 4.7 multiply_convert_fusion
  (395 shorter events, 123.7 us)
Async XLA Ops:
  203.1 33.6 %collective-permute-start = (f32[1,8,4,9,128]{4,2,1,0,3:T(4,128)}, f32[1,8,4,9,128]{4,2,1,0,3:T(4,128)}, u32[]{:S(2)}, u32[]{:S(2)}) collective-permute-start(f32[1,8,4,9,128]{4,2,1,0,3:T(4,128)} %get-tuple-element.46), channel_id=1, source_target_pairs={{0,32},{32,64},{64,96},{96,0},{1,33},{33,65},{65,97},{97,1},{2,34}... | collective-permute-start | bytes 442376 | tf_op jit(solution)/shard_map/ppermute | solution.py:15
  205.7 28.9 %collective-permute-start.1 = (f32[2,1,4,9,128]{4,2,1,0,3:T(4,128)}, f32[2,1,4,9,128]{4,2,1,0,3:T(4,128)}, u32[]{:S(2)}, u32[]{:S(2)}) collective-permute-start(f32[2,1,4,9,128]{4,2,1,0,3:T(4,128)} %slice_bitcast_fusion.43), channel_id=1, source_target_pairs={{0,8},{8,16},{16,24},{24,0},{1,9},{9,17},{17,25},{25,1},{2,10},{10... | collective-permute-start | bytes 110600 | tf_op jit(solution)/shard_map/ppermute | solution.py:15
  208.2 27.4 %collective-permute-start.2 = (f32[2,8,1,9,128]{4,2,1,0,3:T(1,128)}, f32[2,8,1,9,128]{4,2,1,0,3:T(1,128)}, u32[]{:S(2)}, u32[]{:S(2)}) collective-permute-start(f32[2,8,1,9,128]{4,2,1,0,3:T(1,128)} %slice_bitcast_fusion.35), channel_id=1, source_target_pairs={{0,1},{1,2},{2,3},{3,4},{4,5},{5,6},{6,7},{7,0},{8,9},{9,10},{10,1... | collective-permute-start | bytes 221192 | tf_op jit(solution)/shard_map/ppermute | solution.py:15
  222.0 8.5 %collective-permute-start.3 = (f32[1,8,4,9,1]{3,1,2,0,4:T(8,128)}, f32[1,8,4,9,1]{3,1,2,0,4:T(8,128)}, u32[]{:S(2)}, u32[]{:S(2)}) collective-permute-start(f32[1,8,4,9,1]{3,1,2,0,4:T(8,128)} %bitcast.321), channel_id=1, source_target_pairs={{0,32},{32,64},{64,96},{96,0},{1,33},{33,65},{65,97},{97,1},{2,34}... | collective-permute-start | bytes 3464 | tf_op jit(solution)/shard_map/ppermute | solution.py:15
  223.8 5.3 collective-permute-start.4
  241.6 5.8 collective-permute-start.7
  242.8 7.1 %collective-permute-start.6 = (f32[1,8,4,9,128]{4,2,1,0,3:T(4,128)S(1)}, f32[1,8,4,9,128]{4,2,1,0,3:T(4,128)S(1)}, u32[]{:S(2)}, u32[]{:S(2)}) collective-permute-start(f32[1,8,4,9,128]{4,2,1,0,3:T(4,128)S(1)} %get-tuple-element.45), channel_id=1, source_target_pairs={{0,96},{32,0},{64,32},{96,64},{1,97},{33,1},{65,33},{97,65},{2,98}... | collective-permute-start | bytes 442376 | tf_op jit(solution)/shard_map/ppermute | solution.py:15
  244.6 5.2 collective-permute-start.8
  254.7 4.1 collective-permute-start.10
  255.3 5.3 collective-permute-start.9
  255.4 3.8 collective-permute-start.11
  403.9 7.1 %collective-permute-start.12 = (f32[1,8,4,9,128]{4,2,1,0,3:T(4,128)S(1)}, f32[1,8,4,9,128]{4,2,1,0,3:T(4,128)S(1)}, u32[]{:S(2)}, u32[]{:S(2)}) collective-permute-start(f32[1,8,4,9,128]{4,2,1,0,3:T(4,128)S(1)} %get-tuple-element.41), channel_id=1, source_target_pairs={{0,96},{32,0},{64,32},{96,64},{1,97},{33,1},{65,33},{97,65},{2,98}... | collective-permute-start | bytes 442376 | tf_op jit(solution)/shard_map/ppermute | solution.py:15
  404.5 4.2 collective-permute-start.13
  407.1 3.8 collective-permute-start.14
  415.8 4.6 collective-permute-start.16
  416.0 6.0 collective-permute-start.15
  416.3 4.3 collective-permute-start.17
  565.3 4.1 collective-permute-start.19
  566.0 6.1 collective-permute-start.18
  576.9 4.1 collective-permute-start.22
  577.2 5.6 collective-permute-start.21
  653.5 7.9 %collective-permute-start.25 = (f32[2,1,4,9,128]{4,2,1,0,3:T(4,128)S(1)}, f32[2,1,4,9,128]{4,2,1,0,3:T(4,128)S(1)}, u32[]{:S(2)}, u32[]{:S(2)}) collective-permute-start(f32[2,1,4,9,128]{4,2,1,0,3:T(4,128)S(1)} %slice_bitcast_fusion.36), channel_id=1, source_target_pairs={{0,24},{8,0},{16,8},{24,16},{1,25},{9,1},{17,9},{25,17},{2,26},{10... | collective-permute-start | bytes 110600 | tf_op jit(solution)/shard_map/ppermute | solution.py:15
  658.8 5.6 collective-permute-start.24
  660.2 4.1 collective-permute-start.26
  (90 other events, 835.5 us)
where the time goes:
time: 690 us; the launch traced here: 682 us
  blocking collectives  325 us (47%)
  other arithmetic  214 us (31%)
  matrix products  43.4 us (6%)
  local copies, waits for them, and re-layouts  41.3 us (6%)
  starting transfers between devices  33.1 us (5%)
  waiting for transfers between devices  21.7 us (3%)
    psum x5, blocking collectives, global_sum(): return lax.psum(local_value, ('gx', 'gy', 'gz'))  325 us
    another operation x4, other arithmetic, element_blocks(): factor = jnp.linalg.cholesky(schur)  160 us
    ppermute x27, starting transfers between devices, passed_along(): return lax.ppermute(value, axis, pairs)  33.1 us
    ppermute x27, waiting for transfers between devices, passed_along(): return lax.ppermute(value, axis, pairs)  21.7 us
  transfers between devices with their start and end apart: 27, of which 12 were waited for; matrix products, arithmetic and copies ran while one was open for 4% of the time, Pallas kernels for 0%

commit v1 on v0

v1 whole, which is shorter than its diff:
```python
import functools

import jax
import jax.numpy as jnp
from jax import lax
from jax.experimental import pallas as pl
from jax.experimental.pallas import tpu as pltpu
from jax.sharding import PartitionSpec as P

MESH = pl.DeviceIdType.MESH
BF16 = jnp.bfloat16
F32 = jnp.float32

COLS = 128
PRESS = 27
FLUX = 108
BX, BY, BZ = 2, 8, 4
ELEMENTS = BX * BY * BZ

TR = 64
PR = 32

GROUP = 72
X_GROUPS = 0
Y_GROUPS = 12
Z_GROUPS = 21
GROUPS = 31
FIELD = GROUPS * GROUP

BLOCKED = 1e30


def dot3(a, b):
    return jnp.dot(a, b, precision=lax.Precision.HIGH, preferred_element_type=F32)


def lanes_of(shape):
    return lax.broadcasted_iota(jnp.int32, shape, len(shape) - 1)


def packed_pair(value):
    lane = lanes_of(value.shape)
    high = value.astype(BF16).astype(F32)
    low = value - high
    first = jnp.where(lane < 64, high, pltpu.roll(high, 64, 1))
    second = jnp.where(lane < 64, low, jnp.where(lane < 96, high, pltpu.roll(low, 32, 1)))
    return first.astype(BF16), second.astype(BF16)


def blocks_kernel(
    rock, geometry, permeability, mass_inv, div_map, trace_map,
    lmat, hmat,
    joined, joined_t, mass, scale, scale_t, fluxes, coupled, table, inverse,
):
    joined[...] = jnp.zeros_like(joined)
    mass[...] = jnp.zeros_like(mass)
    scale[...] = jnp.zeros_like(scale)
    inverse[...] = jnp.zeros_like(inverse)
    mass[0:FLUX, 0:FLUX] = mass_inv[...]
    for facet in range(6):
        joined[8 * facet : 8 * facet + 8, 0:FLUX] = trace_map[9 * facet : 9 * facet + 8, :]
        joined[48 + facet : 49 + facet, 0:FLUX] = trace_map[9 * facet + 8 : 9 * facet + 9, :]
    joined[TR : TR + PRESS, 0:FLUX] = div_map[...]
    joined_t[...] = jnp.transpose(joined[...])

    rooted = jnp.sqrt(permeability[...])
    lane = lanes_of((16, FLUX))
    per_class = jnp.where(
        lane < 36, rooted[:, 0:1], jnp.where(lane < 72, rooted[:, 1:2], rooted[:, 2:3])
    )
    table[0:16, 0:FLUX] = per_class
    for e in range(ELEMENTS):
        i, j, k = e // 32, (e // 4) % 8, e % 4
        row = table[pl.ds(rock[i, j, k], 1), :][:, 0:FLUX]
        scale[e : e + 1, 0:FLUX] = geometry[i, j, k : k + 1, :] * row
    scale_t[...] = jnp.transpose(scale[...])

    @pl.loop(0, ELEMENTS // 8)
    def build(step):
        turned = pltpu.roll(scale_t[...], lax.rem(128 - 8 * step, 128), 1)
        for pair in range(4):
            e = step * 8 + 2 * pair
            first = jnp.broadcast_to(turned[:, 2 * pair : 2 * pair + 1], (128, 128))
            second = jnp.broadcast_to(turned[:, 2 * pair + 1 : 2 * pair + 2], (128, 128))
            columns = jnp.concatenate([first, second], axis=1)
            both = jnp.concatenate([joined_t[...], joined_t[...]], axis=1)
            flux_side = columns * dot3(mass[...], columns * both)
            pair_coupled = dot3(joined[0:96, :], flux_side)
            fluxes[e] = flux_side[0:112, 0:128]
            fluxes[e + 1] = flux_side[0:112, 128:256]
            coupled[pl.ds(pl.multiple_of(e * 96, 96), 96), :] = pair_coupled[:, 0:128]
            coupled[pl.ds(pl.multiple_of((e + 1) * 96, 96), 96), :] = pair_coupled[:, 128:256]

    half = lanes_of((PR, 128)) < 64
    rows = lax.broadcasted_iota(jnp.int32, (PR, 128), 0)

    def with_schur(table_t):
        for pair in range(14):
            first = coupled[pl.ds(TR + 2 * pair, ELEMENTS, stride=96), :]
            second = coupled[pl.ds(TR + 2 * pair + 1, ELEMENTS, stride=96), :]
            turned = jnp.transpose(jnp.concatenate([first, second], axis=0))[TR : TR + PR, :]
            table_t[2 * pair] = turned
            table_t[2 * pair + 1] = pltpu.roll(turned, 64, 1)

        @pl.loop(0, PRESS)
        def eliminate(k):
            mine = rows == k
            pivot = 1.0 / table_t[k, pl.ds(k, 1), :]
            row = jnp.where(mine, 1.0, table_t[k]) * pivot
            for i in range(PRESS):
                factor = table_t[i, pl.ds(k, 1), :]
                table_t[i] = jnp.where(mine, 0.0, table_t[i]) - factor * row
            table_t[k] = row

        table_t[PRESS] = jnp.zeros((PR, 128), F32)
        for pair in range(14):
            both = jnp.where(half, table_t[2 * pair], pltpu.roll(table_t[2 * pair + 1], 64, 1))
            placed = jnp.concatenate(
                [jnp.zeros((TR, 128), F32), both, jnp.zeros((128 - TR - PR, 128), F32)], axis=0
            )
            turned = jnp.transpose(placed)
            inverse[pl.ds(2 * pair, ELEMENTS, stride=PR), :] = turned[0:ELEMENTS]
            inverse[pl.ds(2 * pair + 1, ELEMENTS, stride=PR), :] = turned[ELEMENTS:]

    pl.run_scoped(with_schur, pltpu.VMEM((28, PR, 128), F32))

    @pl.loop(0, ELEMENTS // 4)
    def finish(step):
        for u in range(4):
            e = step * 4 + u
            full = coupled[pl.ds(pl.multiple_of(e * 96, 96), 96), :]
            inv = inverse[pl.ds(pl.multiple_of(e * PR, PR), PR), :]
            padded = jnp.concatenate([full, jnp.zeros((32, 128), F32)], axis=0)
            solved = jnp.where(lanes_of((PR, 128)) < TR, dot3(inv, padded), inv)
            right = jnp.concatenate(
                [jnp.zeros((TR, 128), F32), solved, jnp.zeros((128 - TR - PR, 128), F32)], axis=0
            )
            flux_side = fluxes[e]
            left = jnp.concatenate([full[0:TR], flux_side], axis=0)
            term = dot3(left, right)
            traced = lanes_of((TR, 128)) < TR
            operator = jnp.where(traced, full[0:TR] - term[0:TR], term[0:TR])
            traced = lanes_of((112, 128)) < TR
            recovery = jnp.where(traced, term[TR:] - flux_side, term[TR:])
            one, two = packed_pair(operator)
            lmat[e, :, 0:128] = one
            lmat[e, :, 128:256] = two
            one, two = packed_pair(recovery)
            hmat[e, :, 0:128] = one
            hmat[e, :, 128:256] = two


def element_blocks(rock_class, geometry, permeability, mass_inv, div_map, trace_map):
    return pl.pallas_call(
        blocks_kernel,
        out_shape=(
            jax.ShapeDtypeStruct((ELEMENTS, TR, 256), BF16),
            jax.ShapeDtypeStruct((ELEMENTS, 112, 256), BF16),
        ),
        in_specs=[pl.BlockSpec(memory_space=pltpu.SMEM)] + [pl.BlockSpec(memory_space=pltpu.VMEM)] * 5,
        out_specs=[pl.BlockSpec(memory_space=pltpu.VMEM)] * 2,
        scratch_shapes=[
            pltpu.VMEM((128, 128), F32),
            pltpu.VMEM((128, 128), F32),
            pltpu.VMEM((128, 128), F32),
            pltpu.VMEM((128, 128), F32),
            pltpu.VMEM((128, 128), F32),
            pltpu.VMEM((ELEMENTS, 112, 128), F32),
            pltpu.VMEM((ELEMENTS * 96, 128), F32),
            pltpu.VMEM((16, 128), F32),
            pltpu.VMEM((ELEMENTS * PR, 128), F32),
        ],
        compiler_params=pltpu.CompilerParams(vmem_limit_bytes=48 * 1024 * 1024),
        name="blocks",
    )(rock_class, geometry, permeability, mass_inv, div_map, trace_map)


def facet_rows(g, i, jj, k):
    slot_x, slot_y, slot_z = jj * 4 + k, i * 4 + k, 2 * g + jj
    places = []
    for side in range(2):
        for group, slot in (
            (X_GROUPS + (i + side) * 4 + g, slot_x),
            (Y_GROUPS + 2 * g + jj + side, slot_y),
            (Z_GROUPS + 2 * (k + side) + i, slot_z),
        ):
            places.append((pl.multiple_of(group * GROUP + slot * 8, 8), group * GROUP + 64 + slot))
    return places


def gathered(field, places):
    row = lax.broadcasted_iota(jnp.int32, (8, COLS), 0)
    ninth = jnp.zeros((8, COLS), F32)
    pieces = []
    for facet, (main, extra) in enumerate(places):
        pieces.append(field[pl.ds(main, 8), :])
        line = jnp.broadcast_to(field[pl.ds(extra, 1), :], (8, COLS))
        ninth = jnp.where(row == facet, line, ninth)
    return pieces + [ninth]


def weights_of(pieces):
    vector = jnp.concatenate(pieces + [jnp.zeros((8, COLS), F32)], axis=0)
    high = vector.astype(BF16)
    low = (vector - high.astype(F32)).astype(BF16)
    return jnp.concatenate([high, low, high], axis=0)


def forcing_of(values):
    padded = jnp.concatenate([values.astype(F32), jnp.zeros((PR - PRESS, COLS), F32)], axis=0)
    padded = padded.astype(BF16)
    return jnp.concatenate([padded, padded], axis=0)


def scatter(values, low, up, places, lift=None):
    for facet, (main, extra) in enumerate(places):
        target = low if facet < 3 else up
        first = values[8 * facet : 8 * facet + 8]
        last = values[48 + facet : 49 + facet]
        if lift is not None and facet < 3:
            first = first + lift[facet]
            last = last + lift[facet]
        target[pl.ds(main, 8), :] = first
        target[pl.ds(extra, 1), :] = last


COPIES = 12


def solver_kernel(
    sizes, dirichlet, lmat, sources, out,
    low, up, inverse, fields, mine, parts_x, parts_y, parts_z,
    send, recv, send_sum, recv_sum,
):
    nx, ny, nz = sizes
    ix, iy, iz = lax.axis_index("gx"), lax.axis_index("gy"), lax.axis_index("gz")

    def at_x(step):
        return (lax.rem(ix + step + nx, nx), iy, iz)

    def at_y(step):
        return (ix, lax.rem(iy + step + ny, ny), iz)

    def at_z(step):
        return (ix, iy, lax.rem(iz + step + nz, nz))

    partners = (
        [at_x(s) for s in range(1, nx)] + [at_y(s) for s in range(1, ny)] + [at_z(s) for s in range(1, nz)]
    )
    barrier = pltpu.get_barrier_semaphore()
    for partner in partners:
        pl.semaphore_signal(barrier, inc=1, device_id=partner, device_id_type=MESH)

    def copy(buffer, stage, slot, source, target, count, device):
        return pltpu.make_async_remote_copy(
            src_ref=buffer.at[stage, pl.ds(source * GROUP, count * GROUP)],
            dst_ref=buffer.at[stage, pl.ds(target * GROUP, count * GROUP)],
            send_sem=send.at[stage, slot],
            recv_sem=recv.at[stage, slot],
            device_id=device,
            device_id_type=MESH,
        )

    def copy_x(stage, g):
        return [
            copy(low, stage, g, X_GROUPS + g, X_GROUPS + 8 + g, 1, at_x(-1)),
            copy(up, stage, 4 + g, X_GROUPS + 8 + g, X_GROUPS + g, 1, at_x(1)),
        ]

    def copy_yz(stage):
        return [
            copy(low, stage, 8, Y_GROUPS, Y_GROUPS + 8, 1, at_y(-1)),
            copy(up, stage, 9, Y_GROUPS + 8, Y_GROUPS, 1, at_y(1)),
            copy(low, stage, 10, Z_GROUPS, Z_GROUPS + 8, 2, at_z(-1)),
            copy(up, stage, 11, Z_GROUPS + 8, Z_GROUPS, 2, at_z(1)),
        ]

    def wait(stage):
        for g in range(4):
            for item in copy_x(stage, g):
                item.wait()
        for item in copy_yz(stage):
            item.wait()

    each = [(i, jj, k) for i in range(BX) for jj in range(2) for k in range(BZ)]

    def element_index(g, i, jj, k):
        return i * 32 + 2 * g * 4 + jj * 4 + k

    lane = lanes_of((TR, 256))
    row = lax.broadcasted_iota(jnp.int32, (TR, 256), 0)
    on_diagonal = (lane == row) | (lane == row + 128)
    ones = jnp.ones((256, COLS), BF16)

    pl.semaphore_wait(barrier, len(partners))

    @pl.loop(0, 4)
    def start(g):
        for i, jj, k in each:
            e = element_index(g, i, jj, k)
            places = facet_rows(g, i, jj, k)
            matrix = lmat[e]
            right = jnp.concatenate([jnp.zeros((192, COLS), BF16), forcing_of(sources[e])], axis=0)
            values = jnp.dot(matrix, right, preferred_element_type=F32)
            scatter(values, low.at[0], up.at[0], places)
            only = jnp.where(on_diagonal, matrix.astype(F32), 0.0).astype(BF16)
            diagonal = jnp.dot(only, ones, preferred_element_type=F32)
            lift = [
                dirichlet[i, 2 * g + jj, k, normal].astype(F32) * BLOCKED for normal in range(3)
            ]
            scatter(diagonal, low.at[1], up.at[1], places, lift)
        for stage in (0, 1):
            for item in copy_x(stage, g):
                item.start()

    for stage in (0, 1):
        for item in copy_yz(stage):
            item.start()
    for stage in (0, 1):
        wait(stage)

    zero = jnp.zeros((8, COLS), F32)

    def begin(group, total):
        for tile in range(9):
            place = pl.ds(pl.multiple_of(group * GROUP + tile * 8, 8), 8)
            diagonal = low[1, place, :] + up[1, place, :]
            scale = jnp.where(diagonal > 0.5 * BLOCKED, 0.0, 1.0 / diagonal)
            inverse[place, :] = scale
            residual = low[0, place, :] + up[0, place, :]
            precond = scale * residual
            fields[0, place, :] = precond
            total = total + residual * precond
        return total

    square = zero
    for first, owned, last in ((0, 8, 12), (12, 20, 21), (21, 29, 31)):
        square = lax.fori_loop(first, owned, begin, square)
        lax.fori_loop(owned, last, begin, zero)

    moments = [square]
    for step in range(3):
        stage = step + 2

        def apply(g, totals):
            totals = list(totals)
            for i, jj, k in each:
                e = element_index(g, i, jj, k)
                places = facet_rows(g, i, jj, k)
                pieces = gathered(fields.at[step], places)
                right = jnp.concatenate([weights_of(pieces), jnp.zeros((64, COLS), BF16)], axis=0)
                values = jnp.dot(lmat[e], right, preferred_element_type=F32)
                others = [pieces]
                if step > 0:
                    others.append(gathered(fields.at[step - 1], places))
                for which, other in enumerate(others):
                    for tile in range(7):
                        totals[which] = totals[which] + other[tile] * values[8 * tile : 8 * tile + 8]
                if step < 2:
                    scatter(values, low.at[stage], up.at[stage], places)
            if step < 2:
                for item in copy_x(stage, g):
                    item.start()
            return tuple(totals)

        totals = lax.fori_loop(0, 4, apply, (zero,) * (1 if step == 0 else 2))
        moments.extend(totals)
        if step < 2:
            for item in copy_yz(stage):
                item.start()
            wait(stage)

            @pl.loop(0, GROUPS)
            def advance(group):
                for tile in range(9):
                    place = pl.ds(pl.multiple_of(group * GROUP + tile * 8, 8), 8)
                    image = low[stage, place, :] + up[stage, place, :]
                    fields[step + 1, place, :] = inverse[place, :] * image - fields[step, place, :]

    sublane = lax.broadcasted_iota(jnp.int32, (8, COLS), 0)
    tile = zero
    for which, moment in enumerate(moments):
        line = jnp.broadcast_to(jnp.sum(moment, axis=0, keepdims=True), (8, COLS))
        tile = jnp.where(sublane == which, line, tile)

    offset = 0
    for stage, (count, at, parts) in enumerate(((nx, at_x, parts_x), (ny, at_y, parts_y), (nz, at_z, parts_z))):
        mine[stage] = tile
        copies = []
        for s in range(1, count):
            copies.append(
                pltpu.make_async_remote_copy(
                    src_ref=mine.at[stage],
                    dst_ref=parts.at[s - 1],
                    send_sem=send_sum.at[offset + s - 1],
                    recv_sem=recv_sum.at[offset + s - 1],
                    device_id=at(s),
                    device_id_type=MESH,
                )
            )
        for item in copies:
            item.start()
        for s, item in enumerate(copies):
            item.wait()
            tile = tile + parts[s]
        offset += count - 1

    b0, g00, g11, g01, g22, g12 = [tile[n : n + 1] for n in range(6)]
    b1 = g00 - b0
    b2 = g01 - b1
    g02 = g11
    l1, l2 = g01 / g00, g02 / g00
    h11, h12, h22 = g11 - l1 * g01, g12 - l1 * g02, g22 - l2 * g02
    d1, d2 = b1 - l1 * b0, b2 - l2 * b0
    sound = h11 > 2e-6 * g11
    m = jnp.where(sound, h12 / h11, 0.0)
    k22 = h22 - m * h12
    c2 = jnp.where(k22 > 2e-6 * g22, (d2 - m * d1) / k22, 0.0)
    c1 = jnp.where(sound, (d1 - h12 * c2) / h11, 0.0)
    c0 = (b0 - g01 * c1 - g02 * c2) / g00
    c0, c1, c2 = [jnp.broadcast_to(c, (8, COLS)) for c in (c0, c1, c2)]

    @pl.loop(0, GROUPS)
    def combine(group):
        for tile in range(9):
            place = pl.ds(pl.multiple_of(group * GROUP + tile * 8, 8), 8)
            out[place, :] = c0 * fields[0, place, :] + c1 * fields[1, place, :] + c2 * fields[2, place, :]


def solve(sizes, dirichlet, lmat, sources):
    partners = sum(sizes) - 3
    return pl.pallas_call(
        functools.partial(solver_kernel, sizes),
        out_shape=jax.ShapeDtypeStruct((FIELD, COLS), F32),
        in_specs=[pl.BlockSpec(memory_space=pltpu.SMEM)] + [pl.BlockSpec(memory_space=pltpu.VMEM)] * 2,
        out_specs=pl.BlockSpec(memory_space=pltpu.VMEM),
        scratch_shapes=[
            pltpu.VMEM((4, FIELD, COLS), F32),
            pltpu.VMEM((4, FIELD, COLS), F32),
            pltpu.VMEM((FIELD, COLS), F32),
            pltpu.VMEM((3, FIELD, COLS), F32),
            pltpu.VMEM((3, 8, COLS), F32),
            pltpu.VMEM((sizes[0] - 1, 8, COLS), F32),
            pltpu.VMEM((sizes[1] - 1, 8, COLS), F32),
            pltpu.VMEM((sizes[2] - 1, 8, COLS), F32),
            pltpu.SemaphoreType.DMA((4, COPIES)),
            pltpu.SemaphoreType.DMA((4, COPIES)),
            pltpu.SemaphoreType.DMA((partners,)),
            pltpu.SemaphoreType.DMA((partners,)),
        ],
        compiler_params=pltpu.CompilerParams(
            collective_id=0, has_side_effects=True, vmem_limit_bytes=48 * 1024 * 1024
        ),
        name="solver",
    )(dirichlet, lmat, sources)


def recover_kernel(field, hmat, sources, traces, flux):
    step = pl.program_id(0)
    i, g = step // 4, lax.rem(step, 4)
    for jj in range(2):
        for k in range(BZ):
            u = jj * 4 + k
            places = facet_rows(g, i, jj, k)
            pieces = gathered(field, places)
            ninth = pieces[6]
            for normal in range(3):
                traces[u, 9 * normal : 9 * normal + 8, :] = pieces[normal]
                traces[u, 9 * normal + 8 : 9 * normal + 9, :] = ninth[normal : normal + 1]
            right = jnp.concatenate([weights_of(pieces), forcing_of(sources[u])], axis=0)
            values = jnp.dot(hmat[u], right, preferred_element_type=F32)
            flux[u] = values[0:FLUX].astype(BF16)


def recover(field, hmat, sources):
    return pl.pallas_call(
        recover_kernel,
        grid=(ELEMENTS // 8,),
        out_shape=(
            jax.ShapeDtypeStruct((ELEMENTS, PRESS, COLS), F32),
            jax.ShapeDtypeStruct((ELEMENTS, FLUX, COLS), BF16),
        ),
        in_specs=[
            pl.BlockSpec((FIELD, COLS), lambda s: (0, 0)),
            pl.BlockSpec((8, 112, 256), lambda s: (s, 0, 0)),
            pl.BlockSpec((8, PRESS, COLS), lambda s: (s, 0, 0)),
        ],
        out_specs=[
            pl.BlockSpec((8, PRESS, COLS), lambda s: (s, 0, 0)),
            pl.BlockSpec((8, FLUX, COLS), lambda s: (s, 0, 0)),
        ],
        compiler_params=pltpu.CompilerParams(vmem_limit_bytes=32 * 1024 * 1024),
        name="recover",
    )(field, hmat, sources)


def body(sizes, sources, geometry, rock_class, permeability, mass_inv, div_map, trace_map, dirichlet):
    forcing = sources.reshape(ELEMENTS, PRESS, COLS)
    lmat, hmat = element_blocks(rock_class, geometry, permeability, mass_inv, div_map, trace_map)
    field = solve(sizes, dirichlet, lmat, forcing)
    traces, flux = recover(field, hmat, forcing)
    return (
        traces.reshape(BX, BY, BZ, PRESS, COLS),
        flux.reshape(BX, BY, BZ, FLUX, COLS),
    )


def solution(mesh):
    sizes = (mesh.shape["gx"], mesh.shape["gy"], mesh.shape["gz"])
    placed = (
        P("gx", "gy", "gz", None, None),
        P("gx", "gy", "gz", None),
        P("gx", "gy", "gz"),
        P(),
        P(),
        P(),
        P(),
        P("gx", "gy", "gz", None),
    )
    return jax.shard_map(
        functools.partial(body, sizes),
        mesh=mesh,
        in_specs=placed,
        out_specs=(P("gx", "gy", "gz", None, None), P("gx", "gy", "gz", None, None)),
        check_vma=False,
    )
```

time: 690 us -> 88.5 us (0.13); the launches traced: 682 us -> 88 us
  blocking collectives: 325 us -> 0 us
  other arithmetic: 214 us -> 0 us
  Pallas kernels: 0 us -> 77.4 us
  matrix products: 43.4 us -> 0 us
  starting transfers between devices: 33.1 us -> 0 us
  local copies, waits for them, and re-layouts: 41.3 us -> 9.9 us
  waiting for transfers between devices: 21.7 us -> 0 us
    psum x5 -> x0, blocking collectives: 325 us -> none  [global_sum(): return lax.psum(local_value, ('gx', 'gy', 'gz'))]
    another operation x43 -> x0, other arithmetic: 179 us -> none  [the longest x4 160 us: element_blocks(): factor = jnp.linalg.cholesky(schur)]
    pallas_call x0 -> x3, Pallas kernels: none -> 77.4 us  [the longest x1 44 us: solve(): pl.pallas_call(functools.partial(solver_kernel, sizes), out_shape=jax.Sha...]
    dot_general x11 -> x0, matrix products: 37.4 us -> none  [the longest x3 9.47 us: body(): jnp.einsum('ets,esr->etr', condensed, operate_values, precision=finest)]
    ppermute x27 -> x0, starting transfers between devices: 33.1 us -> none  [passed_along(): return lax.ppermute(value, axis, pairs)]
    ppermute x27 -> x0, waiting for transfers between devices: 21.7 us -> none  [passed_along(): return lax.ppermute(value, axis, pairs)]
    add x7 -> x0, other arithmetic: 13.4 us -> none  [combine(): return tuple((left + weight * right for left, right in zip(first, second)))]
    reduce_sum x5 -> x0, other arithmetic: 11.2 us -> none  [column_inner(): return jnp.sum(first[0] * second[0], axis=(0, 1, 2, 3, 4))]
  transfers between devices with their start and end apart: 27 -> 0, of which waited for: 12 -> 0; matrix products, arithmetic and copies ran while one was open for 4% -> 0% of each run, Pallas kernels for 0% -> 0%
where the time goes in v1:
time: 88.5 us; the launch traced here: 88 us
  Pallas kernels  77.4 us (87%)
  local copies, waits for them, and re-layouts  9.9 us (11%)
    pallas_call x1, Pallas kernels, solve(): pl.pallas_call(functools.partial(solver_kernel, sizes), out_shape=jax.Sha...  44 us
    pallas_call x1, Pallas kernels, element_blocks(): pl.pallas_call(blocks_kernel, out_shape=(jax.ShapeDtypeStruct((ELEMENTS,...  31.1 us
    unnamed x14, local copies, waits for them, and re-layouts  9.9 us
    pallas_call x1, Pallas kernels, recover(): pl.pallas_call(recover_kernel, grid=(ELEMENTS // 8,), out_shape=(jax.Shap...  2.34 us

profile of v1, /device:TPU:1, one launch (start us, length us, event | category | flops | bytes accessed | tf_op | source)
XLA Modules:
  0.0 88.0 jit_solution(13835185912397407619)
XLA Ops:
  0.6 0.8 copy.10.rock
  1.4 0.8 copy.11.permeability
  2.2 0.8 copy.13.dirichlet
  3.0 1.1 %copy.12 = bf16[2,8,4,27,128]{4,3,2,1,0:T(8,128)(2,1)S(1)} copy(bf16[2,8,4,27,128]{4,2,3,1,0:T(4,128)(2,1)} %param.8) | data formatting | bytes 884736 | tf_op args[0]
  4.1 0.0 copy-start
  4.1 0.8 copy-done
  4.9 0.0 copy-start.1
  4.9 0.8 copy-done.1
  5.7 0.0 copy-start.2
  5.7 0.7 copy-done.2
  6.4 0.0 copy-start.3
  6.4 0.7 copy-done.3
  7.2 31.1 %blocks.1 = (bf16[64,64,256]{2,1,0:T(8,128)(2,1)S(1)}, bf16[64,112,256]{2,1,0:T(8,128)(2,1)S(1)}) custom-call(s32[2,8,4]{2,1,0:T(8,128)S(1)} %copy.10.rock, f32[2,8,4,108]{3,2,1,0:T(4,128)S(1)} %copy-done.1, f32[16,3]{1,0:T(8,128)S(1)} %copy.11.permeability, f32[108,108]{1,0:T(8,128)S(1)} %copy-done, f32[27,108]{1,0:T(8,128)S(1)} %copy-done.3, ...), custom_call_target="tpu_custom_call" | custom-call | tf_op jit(solution)/shard_map/blocks/pallas_call | solution.py:154
  38.2 44.0 %solver.1.field = f32[2232,128]{1,0:T(8,128)S(1)} custom-call(s32[2,8,4,3]{3,2,1,0:T(4,128)S(1)} %copy.13.dirichlet, bf16[64,64,256]{2,1,0:T(8,128)(2,1)S(1)} %get-tuple-element.6.lmat, bf16[64,27,128]{2,1,0:T(8,128)(2,1)S(1)} %bitcast.3), custom_call_target="tpu_custom_call" | custom-call | tf_op jit(solution)/shard_map/solver/pallas_call | solution.py:432
  82.2 2.3 %recover.1 = (f32[64,27,128]{2,1,0:T(8,128)S(1)}, bf16[64,108,128]{2,1,0:T(8,128)(2,1)S(1)}) custom-call(f32[2232,128]{1,0:T(8,128)S(1)} %solver.1.field, bf16[64,112,256]{2,1,0:T(8,128)(2,1)S(1)} %get-tuple-element.7.hmat, bf16[64,27,128]{2,1,0:T(8,128)(2,1)S(1)} %bitcast.4), custom_call_target="tpu_custom_call" | custom-call | tf_op jit(solution)/shard_map/recover/pallas_call | solution.py:476
  84.6 1.5 %copy.14 = f32[2,8,4,27,128]{4,2,3,1,0:T(4,128)} copy(f32[2,8,4,27,128]{4,3,2,1,0:T(8,128)S(1)} %bitcast.6) | data formatting | bytes 1769472
  86.1 1.9 %copy.15 = bf16[2,8,4,108,128]{4,2,3,1,0:T(4,128)(2,1)} copy(bf16[2,8,4,108,128]{4,3,2,1,0:T(8,128)(2,1)S(1)} %bitcast.5) | data formatting | bytes 3538944
Async XLA Ops:
  4.1 0.8 copy-start
  4.9 0.8 copy-start.1
  5.7 0.7 copy-start.2
  6.4 0.7 copy-start.3

commit v2 on v0

v2 whole, which is shorter than its diff:
```python
import functools

import jax
import jax.numpy as jnp
from jax import lax
from jax.experimental import pallas as pl
from jax.experimental.pallas import tpu as pltpu
from jax.sharding import PartitionSpec as P

MESH = pl.DeviceIdType.MESH
BF16 = jnp.bfloat16
F32 = jnp.float32

COLS = 128
PRESS = 27
FLUX = 108
BX, BY, BZ = 2, 8, 4
ELEMENTS = BX * BY * BZ

TR = 64
PR = 32
FR = 112
AR = TR + FR

GROUP = 72
Z_GROUP = 40
Y_START = 12 * GROUP
Z_START = Y_START + 9 * GROUP
FIELD = Z_START + 20 * Z_GROUP

BLOCKED = 1e30
MIB = 1024 * 1024

BATCH = 16


def lanes_of(shape):
    return lax.broadcasted_iota(jnp.int32, shape, len(shape) - 1)


def rows_of(shape):
    return lax.broadcasted_iota(jnp.int32, shape, len(shape) - 2)


def halves(value):
    high = value.astype(BF16)
    return high, (value - high.astype(F32)).astype(BF16)


def blocks_kernel(
    rock, dirichlet, geometry_hbm, permeability_hbm, mass_hbm, div_hbm, trace_hbm, sources_hbm,
    lmat, hmat, forcing, diagonals,
    geometry, permeability, mass_in, div_map, trace_map, sources,
    joined, joined_t, padded, scale_t, left_mass, left_joined,
    highs, lows, press, inverse, table, spread, columns, first, second, solved_in, right, sems,
):
    loads = [
        pltpu.make_async_copy(source, target, sems.at[n])
        for n, (source, target) in enumerate(
            (
                (trace_hbm, trace_map),
                (div_hbm, div_map),
                (mass_hbm, mass_in),
                (permeability_hbm, permeability),
                (geometry_hbm, geometry),
                (sources_hbm, sources),
            )
        )
    ]
    for item in loads:
        item.start()
    joined[...] = jnp.zeros_like(joined)
    padded[...] = jnp.zeros_like(padded)
    inverse[...] = jnp.zeros_like(inverse)
    for item in loads[:4]:
        item.wait()

    for facet in range(6):
        joined[8 * facet : 8 * facet + 8, 0:FLUX] = trace_map[9 * facet : 9 * facet + 8, :]
        joined[48 + facet : 49 + facet, 0:FLUX] = trace_map[9 * facet + 8 : 9 * facet + 9, :]
    joined[TR : TR + PRESS, 0:FLUX] = div_map[...]
    joined[TR + PR : TR + PR + PRESS, 0:FLUX] = div_map[...]
    joined_t[...] = jnp.transpose(joined[...])
    high, low = halves(joined[0 : TR + PR, :])
    left_joined[:, 0:128] = high
    left_joined[:, 128:256] = high
    left_joined[:, 256:384] = low
    padded[0:FLUX, 0:FLUX] = mass_in[...]
    high, low = halves(padded[0:FR, :])
    left_mass[:, 0:128] = high
    left_mass[:, 128:256] = high
    left_mass[:, 256:384] = low

    padded[...] = jnp.zeros_like(padded)
    padded[0:3, 0:16] = jnp.sqrt(permeability[...])
    rooted = jnp.transpose(padded[...])[0:16]
    lane = lanes_of((16, 128))
    table[0:16, :] = jnp.where(
        lane < 36, rooted[:, 0:1], jnp.where(lane < 72, rooted[:, 1:2], rooted[:, 2:3])
    )
    padded[...] = jnp.zeros_like(padded)
    loads[4].wait()
    for e in range(ELEMENTS):
        i, j, k = e // 32, (e // 4) % 8, e % 4
        row = table[pl.ds(rock[i, k, j], 1), :][:, 0:FLUX]
        padded[e : e + 1, 0:FLUX] = geometry[i, j, k : k + 1, :] * row
    scale_t[...] = jnp.transpose(padded[...])

    no_rows = jnp.zeros((128 - FR, 256), BF16)
    for pair in range(BATCH // 2):
        for part in range(3):
            first[pair, 128 * part + FR : 128 * part + 128, :] = no_rows
            second[pair, 128 * part + FR : 128 * part + 128, :] = no_rows

    @pl.loop(0, ELEMENTS // BATCH)
    def build(step):
        turned = pltpu.roll(scale_t[0:FR, :], lax.rem(128 - BATCH * step, 128), 1)
        for pair in range(BATCH // 2):
            for n in range(2):
                column = jnp.broadcast_to(turned[:, 2 * pair + n : 2 * pair + n + 1], (FR, 128))
                cut = slice(128 * n, 128 * n + 128)
                columns[pair, :, cut] = column
                high, low = halves(column * joined_t[0:FR, :])
                first[pair, 0:FR, cut] = high
                first[pair, 128 : 128 + FR, cut] = low
                first[pair, 256 : 256 + FR, cut] = high
        for pair in range(BATCH // 2):
            flux_side = columns[pair] * jnp.dot(left_mass[...], first[pair], preferred_element_type=F32)
            high, low = halves(flux_side)
            second[pair, 0:FR, :] = high
            second[pair, 128 : 128 + FR, :] = low
            second[pair, 256 : 256 + FR, :] = high
            for n in range(2):
                e = step * BATCH + 2 * pair + n
                cut = slice(128 * n, 128 * n + 128)
                highs[e, TR:AR, :] = high[:, cut]
                lows[e, TR:AR, :] = low[:, cut]
        for pair in range(BATCH // 2):
            coupled = jnp.dot(left_joined[...], second[pair], preferred_element_type=F32)
            high, low = halves(coupled[0:TR])
            for n in range(2):
                e = step * BATCH + 2 * pair + n
                cut = slice(128 * n, 128 * n + 128)
                highs[e, 0:TR, :] = high[:, cut]
                lows[e, 0:TR, :] = low[:, cut]
                press[pl.ds(pl.multiple_of(e * PR, PR), PR), :] = coupled[TR:, cut]

    low_half = lanes_of((PR, 128)) < 64
    row_of = rows_of((PR, 128))

    def invert(work):
        for pair in range(14):
            rows = [press[pl.ds(2 * pair + n, ELEMENTS, stride=PR), :] for n in range(2)]
            work[pair] = jnp.transpose(jnp.concatenate(rows, axis=0))[TR : TR + PR, :]

        for k in range(PRESS):
            owner, ahead = k // 2, (k + 1) // 2 % 14
            mine = row_of == k
            held = low_half if k % 2 == 0 else jnp.logical_not(low_half)
            source = work[owner]
            source = jnp.where(held, source, pltpu.roll(source, 64, 1))
            row = jnp.where(mine, 1.0, source) * (1.0 / source[k : k + 1, :])
            for pair in [ahead] + [p for p in range(14) if p != ahead]:
                value = work[pair]
                value = jnp.where(mine, 0.0, value) - value[k : k + 1, :] * row
                work[pair] = jnp.where(held, row, value) if pair == owner else value

        for pair in range(14):
            placed = jnp.concatenate(
                [work[pair], jnp.zeros((PR, 128), F32), work[pair], work[pair]], axis=0
            )
            turned = jnp.transpose(placed)
            inverse[pl.ds(2 * pair, ELEMENTS, stride=PR), :] = turned[0:ELEMENTS]
            inverse[pl.ds(2 * pair + 1, ELEMENTS, stride=PR), :] = turned[ELEMENTS:]

    pl.run_scoped(invert, pltpu.VMEM((14, PR, 128), F32))

    lane = lanes_of((TR, 256))
    unit = jnp.where((jnp.bitwise_and(lane, 63) == rows_of((TR, 256))) & (lane < 192), 1.0, 0.0)
    unit = unit.astype(BF16)
    for u in range(BATCH):
        solved_in[u, PR:TR, :] = jnp.zeros((PR, 128), BF16)
        right[u, 0:64, :] = unit
        right[u, 128:192, :] = unit
        right[u, 224:256, :] = jnp.zeros((PR, 256), BF16)
    lane = lanes_of((PR, 128))
    lane_t = lanes_of((TR, 128))
    on_diagonal = lane_t == rows_of((TR, 128))
    line = lanes_of((1, 128))
    lane_f = lanes_of((AR, 128))
    kept_high = (lane_f >= TR) & (lane_f < TR + PR)
    x_lanes = (line < 8) | (line == 48)
    y_lanes = ((line >= 8) & (line < 16)) | (line == 49)
    z_lanes = ((line >= 16) & (line < 24)) | (line == 50)

    @pl.loop(0, ELEMENTS // BATCH)
    def finish(step):
        for u in range(BATCH):
            e = step * BATCH + u
            high, low = halves(press[pl.ds(pl.multiple_of(e * PR, PR), PR), :])
            solved_in[u, 0:PR, :] = low
            solved_in[u, TR : TR + PR, :] = high
            solved_in[u, TR + PR :, :] = high
        for u in range(BATCH):
            e = step * BATCH + u
            inv = inverse[pl.ds(pl.multiple_of(e * PR, PR), PR), :]
            left = jnp.where(lane < TR + PR, inv, inv - inv.astype(BF16).astype(F32)).astype(BF16)
            solved = jnp.dot(left, solved_in[u], preferred_element_type=F32)
            for part, other in enumerate((pltpu.roll(solved, TR, 1), inv)):
                high, low = halves(-jnp.where(lane < TR, solved, other))
                cut = slice(128 * part, 128 * part + 128)
                right[u, 64:96, cut] = high
                right[u, 96:128, cut] = low
                right[u, 192:224, cut] = high
        for u in range(BATCH):
            e = step * BATCH + u
            left = jnp.concatenate([highs[e], lows[e]], axis=1)
            result = jnp.dot(left, right[u], preferred_element_type=F32)
            both, rest = result[:, 0:128], result[:, 128:256]
            diagonals[pl.ds(e, 1), :] = jnp.sum(
                jnp.where(on_diagonal, both[0:TR], 0.0), axis=0, keepdims=True
            )
            both = both.astype(BF16)
            rest = jnp.where(kept_high, rest, rest - rest.astype(BF16).astype(F32)).astype(BF16)
            lmat[e, :, 0:128] = both[0:TR]
            lmat[e, :, 128:256] = rest[0:TR]
            hmat[e, :, 0:128] = both[TR:]
            hmat[e, :, 128:256] = rest[TR:]

    for e in range(ELEMENTS):
        i, j, k = e // 32, (e // 4) % 8, e % 4
        lift = [dirichlet[i, normal, k, j].astype(F32) * BLOCKED for normal in range(3)]
        diagonals[e : e + 1, :] = diagonals[e : e + 1, :] + jnp.where(
            x_lanes, lift[0], jnp.where(y_lanes, lift[1], jnp.where(z_lanes, lift[2], 0.0))
        )

    loads[5].wait()
    for part in range(4):
        spread[...] = sources[432 * part : 432 * part + 432, :].astype(F32)
        for jj in range(4):
            for k in range(BZ):
                e = part * 16 + jj * 4 + k
                values = spread[pl.ds(108 * jj + k, PRESS, stride=4), :]
                values = jnp.concatenate([values, jnp.zeros((PR - PRESS, COLS), F32)], axis=0)
                forcing[e] = values.astype(BF16)


def element_blocks(rock_class, dirichlet, geometry, permeability, mass_inv, div_map, trace_map, sources):
    smem, hbm, vmem = [
        pl.BlockSpec(memory_space=space) for space in (pltpu.SMEM, pltpu.HBM, pltpu.VMEM)
    ]
    return pl.pallas_call(
        blocks_kernel,
        out_shape=(
            jax.ShapeDtypeStruct((ELEMENTS, TR, 256), BF16),
            jax.ShapeDtypeStruct((ELEMENTS, FR, 256), BF16),
            jax.ShapeDtypeStruct((ELEMENTS, PR, COLS), BF16),
            jax.ShapeDtypeStruct((ELEMENTS, 128), F32),
        ),
        in_specs=[smem] * 2 + [hbm] * 6,
        out_specs=[vmem] * 4,
        scratch_shapes=[
            pltpu.VMEM(geometry.shape, F32),
            pltpu.VMEM(permeability.shape, F32),
            pltpu.VMEM(mass_inv.shape, F32),
            pltpu.VMEM(div_map.shape, F32),
            pltpu.VMEM(trace_map.shape, F32),
            pltpu.VMEM(sources.shape, BF16),
            pltpu.VMEM((128, 128), F32),
            pltpu.VMEM((128, 128), F32),
            pltpu.VMEM((128, 128), F32),
            pltpu.VMEM((128, 128), F32),
            pltpu.VMEM((FR, 384), BF16),
            pltpu.VMEM((TR + PR, 384), BF16),
            pltpu.VMEM((ELEMENTS, AR, 128), BF16),
            pltpu.VMEM((ELEMENTS, AR, 128), BF16),
            pltpu.VMEM((ELEMENTS * PR, 128), F32),
            pltpu.VMEM((ELEMENTS * PR, 128), F32),
            pltpu.VMEM((16, 128), F32),
            pltpu.VMEM((432, 128), F32),
            pltpu.VMEM((BATCH // 2, FR, 256), F32),
            pltpu.VMEM((BATCH // 2, 384, 256), BF16),
            pltpu.VMEM((BATCH // 2, 384, 256), BF16),
            pltpu.VMEM((BATCH, 128, 128), BF16),
            pltpu.VMEM((BATCH, 256, 256), BF16),
            pltpu.SemaphoreType.DMA((6,)),
        ],
        compiler_params=pltpu.CompilerParams(vmem_limit_bytes=28 * MIB),
        name="blocks",
    )(rock_class, dirichlet, geometry, permeability, mass_inv, div_map, trace_map, sources)


def facet_rows(g, i, jj, k):
    places = []
    for side in range(2):
        for start, size, slot in (
            (((i + side) * 4 + g) * GROUP, 64, jj * 4 + k),
            (Y_START + (2 * g + jj + side) * GROUP, 64, i * 4 + k),
            (Z_START + ((k + side) * 4 + g) * Z_GROUP, 32, i * 2 + jj),
        ):
            places.append((pl.multiple_of(start + slot * 8, 8), start + size + slot))
    return places


def gathered(field, places):
    row = rows_of((8, COLS))
    ninth = jnp.zeros((8, COLS), F32)
    pieces = []
    for facet, (main, extra) in enumerate(places):
        pieces.append(field[pl.ds(main, 8), :])
        line = jnp.broadcast_to(field[pl.ds(extra, 1), :], (8, COLS))
        ninth = jnp.where(row == facet, line, ninth)
    return pieces + [ninth]


def scatter(values, low, up, places):
    for facet, (main, extra) in enumerate(places):
        target = low if facet < 3 else up
        target[pl.ds(main, 8), :] = values[8 * facet : 8 * facet + 8]
        target[pl.ds(extra, 1), :] = values[48 + facet : 49 + facet]


EACH = [(i, jj, k) for i in range(BX) for jj in range(2) for k in range(BZ)]


def element_index(g, i, jj, k):
    return i * 32 + g * 8 + jj * 4 + k


def solver_kernel(
    sizes, diagonals, lmat, forcing, vectors, scales,
    low, up, inverse, fields, weights, near, turned, mine, parts_x, parts_y, parts_z,
    send, recv, send_y, recv_y, send_d, recv_d, send_sum, recv_sum,
):
    nx, ny, nz = sizes
    ix, iy, iz = lax.axis_index("gx"), lax.axis_index("gy"), lax.axis_index("gz")

    def at_x(step):
        return (lax.rem(ix + step + nx, nx), iy, iz)

    def at_y(step):
        return (ix, lax.rem(iy + step + ny, ny), iz)

    def at_z(step):
        return (ix, iy, lax.rem(iz + step + nz, nz))

    partners = (
        [at_x(s) for s in range(1, nx)] + [at_y(s) for s in range(1, ny)] + [at_z(s) for s in range(1, nz)]
    )
    barrier = pltpu.get_barrier_semaphore()
    for partner in partners:
        pl.semaphore_signal(barrier, inc=1, device_id=partner, device_id_type=MESH)

    zero = jnp.zeros((8, COLS), F32)
    for u in range(len(EACH)):
        weights[u, 3 * TR : 4 * TR, :] = jnp.zeros((TR, COLS), BF16)

    @pl.loop(0, 16)
    def clear(group):
        for stage in range(3):
            start = Z_START + 32 + group * Z_GROUP
            low[stage, pl.ds(pl.multiple_of(start, 8), 8), :] = zero
            up[stage, pl.ds(pl.multiple_of(start + 4 * Z_GROUP, 8), 8), :] = zero

    @pl.loop(0, 20)
    def clear_inverse(group):
        inverse[pl.ds(pl.multiple_of(Z_START + 32 + group * Z_GROUP, 8), 8), :] = zero

    def remote(source, target, sent, received, device):
        return pltpu.make_async_remote_copy(
            src_ref=source, dst_ref=target, send_sem=sent, recv_sem=received,
            device_id=device, device_id_type=MESH,
        )

    def field_copy(buffer, stage, source, target, count, sent, received, device):
        return remote(
            buffer.at[stage, pl.ds(pl.multiple_of(source, 8), count)],
            buffer.at[stage, pl.ds(pl.multiple_of(target, 8), count)],
            sent, received, device,
        )

    def copies_xz(stage, g):
        x, z = g * GROUP, Z_START + g * Z_GROUP
        x_last, z_last = x + 8 * GROUP, z + 16 * Z_GROUP
        return [
            field_copy(low, stage, x, x_last, GROUP, send.at[stage, 0, g], recv.at[stage, 0, g], at_x(-1)),
            field_copy(up, stage, x_last, x, GROUP, send.at[stage, 1, g], recv.at[stage, 1, g], at_x(1)),
            field_copy(low, stage, z, z_last, Z_GROUP, send.at[stage, 2, g], recv.at[stage, 2, g], at_z(-1)),
            field_copy(up, stage, z_last, z, Z_GROUP, send.at[stage, 3, g], recv.at[stage, 3, g], at_z(1)),
        ]

    def copy_y(stage, side):
        first, last = Y_START, Y_START + 8 * GROUP
        if side == 0:
            return field_copy(low, stage, first, last, GROUP, send_y.at[stage, 0], recv_y.at[stage, 0], at_y(-1))
        return field_copy(up, stage, last, first, GROUP, send_y.at[stage, 1], recv_y.at[stage, 1], at_y(1))

    pl.semaphore_wait(barrier, len(partners))

    half = ELEMENTS // 2
    near_copies = [
        remote(diagonals.at[pl.ds(half, half)], near.at[0, pl.ds(0, half)], send_d.at[0], recv_d.at[0], at_x(1)),
        remote(diagonals.at[pl.ds(0, half)], near.at[1, pl.ds(0, half)], send_d.at[1], recv_d.at[1], at_x(-1)),
        remote(diagonals, near.at[2], send_d.at[2], recv_d.at[2], at_y(1)),
        remote(diagonals, near.at[3], send_d.at[3], recv_d.at[3], at_y(-1)),
        remote(diagonals, near.at[4], send_d.at[4], recv_d.at[4], at_z(1)),
        remote(diagonals, near.at[5], send_d.at[5], recv_d.at[5], at_z(-1)),
    ]
    for item in near_copies:
        item.start()

    def order(n):
        return lax.rem(3 * n, 4)

    def send_chunk(stage, n):
        for item in copies_xz(stage, order(n)):
            item.start()
        for side in range(2):
            @pl.when(n == side)
            def _():
                copy_y(stage, side).start()

    @pl.loop(0, 4)
    def start(n):
        g = order(n)
        for i, jj, k in EACH:
            e = element_index(g, i, jj, k)
            right = jnp.concatenate([jnp.zeros((TR, COLS), BF16), forcing[e], forcing[e]], axis=0)
            values = -jnp.dot(lmat[e, :, 128:256], right, preferred_element_type=F32)
            scatter(values, low.at[0], up.at[0], facet_rows(g, i, jj, k))
        send_chunk(0, n)

    for item in near_copies:
        item.wait()
    lane, row = lanes_of((ELEMENTS, 128)), rows_of((ELEMENTS, 128))
    x_lanes = (lane < 8) | (lane == 48)
    y_lanes = ((lane >= 8) & (lane < 16)) | (lane == 49)

    def uppers(value):
        return jnp.where(lane < 24, pltpu.roll(value, 104, 1), pltpu.roll(value, 125, 1))

    def reciprocal(total):
        return jnp.where(total > 0.5 * BLOCKED, 0.0, 1.0 / total)

    own = diagonals[...]
    own_up = uppers(own)
    from_x = jnp.concatenate([uppers(near[0])[0:half], own_up[0:half]], axis=0)
    first_y, first_z = jnp.bitwise_and(row, 31) < 4, jnp.bitwise_and(row, 3) == 0
    from_y = jnp.where(first_y, pltpu.roll(uppers(near[2]), 36, 0), pltpu.roll(own_up, 4, 0))
    from_z = jnp.where(first_z, pltpu.roll(uppers(near[4]), 61, 0), pltpu.roll(own_up, 1, 0))
    lower_sum = own + jnp.where(x_lanes, from_x, jnp.where(y_lanes, from_y, from_z))
    above_x = jnp.concatenate([near[1, 0:half, :], near[1, 0:half, :]], axis=0)
    above_y, above_z = pltpu.roll(near[3], 28, 0), pltpu.roll(near[5], 3, 0)
    upper_sum = own_up + jnp.where(x_lanes, above_x, jnp.where(y_lanes, above_y, above_z))
    flipped = jnp.transpose(jnp.concatenate([reciprocal(lower_sum), reciprocal(upper_sum)], axis=0))
    turned[0:24, :] = flipped[0:24]
    turned[24:32, :] = flipped[48:56]

    @pl.loop(0, 4)
    def expand(g):
        rolled = pltpu.roll(turned[...], lax.rem(128 - 8 * g, 128), 1)
        for i, jj, k in EACH:
            column = i * 32 + jj * 4 + k
            places = facet_rows(g, i, jj, k)
            for side in range(2):
                normals = [0, 1, 2] if side == 0 else [n for n, last in enumerate((i == 1, jj == 1, k == 3)) if last]
                if not normals:
                    continue
                at = 64 * side + column
                ninth = jnp.broadcast_to(rolled[24:32, at : at + 1], (8, COLS))
                for normal in normals:
                    main, extra = places[3 * side + normal]
                    inverse[pl.ds(main, 8), :] = jnp.broadcast_to(
                        rolled[8 * normal : 8 * normal + 8, at : at + 1], (8, COLS)
                    )
                    inverse[pl.ds(extra, 1), :] = ninth[normal : normal + 1]

    def update(step, g, total):
        spans = [((plane * 4 + g) * GROUP, 9, plane < 2) for plane in range(3)]
        spans += [(Y_START + (2 * g + plane) * GROUP, 9, plane < 2) for plane in range(3)]
        spans += [(Z_START + (plane * 4 + g) * Z_GROUP, 5, plane < 4) for plane in range(5)]
        for begin, tiles, owned in spans:
            for tile in range(tiles):
                place = pl.ds(pl.multiple_of(begin + tile * 8, 8), 8)
                value = low[step, place, :] + up[step, place, :]
                scaled = inverse[place, :] * value
                if step == 0:
                    fields[0, place, :] = scaled
                    if owned:
                        total = total + value * scaled
                else:
                    fields[step, place, :] = scaled - fields[step - 1, place, :]
        return total

    def operate(step, n, totals):
        g = order(n)
        totals = list(totals)
        for item in copies_xz(step, g):
            item.wait_recv()
        for side in range(2):
            @pl.when(n == 1 - side)
            def _():
                copy_y(step, side).wait_recv()
        totals[0] = update(step, g, totals[0])
        for u, (i, jj, k) in enumerate(EACH):
            pieces = gathered(fields.at[step], facet_rows(g, i, jj, k))
            vector = jnp.concatenate(pieces + [jnp.zeros((8, COLS), F32)], axis=0)
            vectors[step, element_index(g, i, jj, k)] = vector
            high, low_part = halves(vector)
            weights[u, 0:TR, :] = high
            weights[u, TR : 2 * TR, :] = low_part
            weights[u, 2 * TR : 3 * TR, :] = high
        for u, (i, jj, k) in enumerate(EACH):
            e = element_index(g, i, jj, k)
            values = jnp.dot(lmat[e], weights[u], preferred_element_type=F32)
            for which in range(1 if step == 0 else 2):
                products = vectors[step - which, e] * values
                parts = [products[8 * tile : 8 * tile + 8] for tile in range(7)]
                part = (parts[0] + parts[1]) + (parts[2] + parts[3])
                part = part + ((parts[4] + parts[5]) + parts[6])
                totals[1 + which] = totals[1 + which] + part
            if step < 2:
                scatter(values, low.at[step + 1], up.at[step + 1], facet_rows(g, i, jj, k))
        if step < 2:
            send_chunk(step + 1, n)
        return tuple(totals)

    moments = []
    for step in range(3):
        totals = lax.fori_loop(0, 4, functools.partial(operate, step), (zero,) * 3)
        moments += [totals[:2], totals[1:], totals[1:]][step]

    sublane = rows_of((8, COLS))
    tile = zero
    for which, moment in enumerate(moments):
        line = jnp.broadcast_to(jnp.sum(moment, axis=0, keepdims=True), (8, COLS))
        tile = jnp.where(sublane == which, line, tile)

    offset = 0
    for stage, (count, at, parts) in enumerate(((nx, at_x, parts_x), (ny, at_y, parts_y), (nz, at_z, parts_z))):
        mine[stage] = tile
        copies = [
            remote(mine.at[stage], parts.at[s - 1], send_sum.at[offset + s - 1], recv_sum.at[offset + s - 1], at(s))
            for s in range(1, count)
        ]
        for item in copies:
            item.start()
        for s, item in enumerate(copies):
            item.wait()
            tile = tile + parts[s]
        offset += count - 1

    b0, g00, g11, g01, g22, g12 = [tile[n : n + 1] for n in range(6)]
    b1 = g00 - b0
    b2 = g01 - b1
    g02 = g11
    l1, l2 = g01 / g00, g02 / g00
    h11, h12, h22 = g11 - l1 * g01, g12 - l1 * g02, g22 - l2 * g02
    d1, d2 = b1 - l1 * b0, b2 - l2 * b0
    sound = h11 > 2e-6 * g11
    m = jnp.where(sound, h12 / h11, 0.0)
    k22 = h22 - m * h12
    c2 = jnp.where(k22 > 2e-6 * g22, (d2 - m * d1) / k22, 0.0)
    c1 = jnp.where(sound, (d1 - h12 * c2) / h11, 0.0)
    c0 = (b0 - g01 * c1 - g02 * c2) / g00
    for n, c in enumerate((c0, c1, c2)):
        scales[8 * n : 8 * n + 8, :] = jnp.broadcast_to(c, (8, COLS))

    @pl.loop(0, 4)
    def drain(g):
        for stage in range(3):
            for item in copies_xz(stage, g):
                item.wait_send()

    for stage in range(3):
        for side in range(2):
            copy_y(stage, side).wait_send()


def solve(sizes, diagonals, lmat, forcing):
    partners = sum(sizes) - 3
    return pl.pallas_call(
        functools.partial(solver_kernel, sizes),
        out_shape=(
            jax.ShapeDtypeStruct((3, ELEMENTS, TR, COLS), F32),
            jax.ShapeDtypeStruct((24, COLS), F32),
        ),
        in_specs=[pl.BlockSpec(memory_space=pltpu.VMEM)] * 3,
        out_specs=[pl.BlockSpec(memory_space=pltpu.VMEM)] * 2,
        scratch_shapes=[
            pltpu.VMEM((3, FIELD, COLS), F32),
            pltpu.VMEM((3, FIELD, COLS), F32),
            pltpu.VMEM((FIELD, COLS), F32),
            pltpu.VMEM((3, FIELD, COLS), F32),
            pltpu.VMEM((len(EACH), 256, COLS), BF16),
            pltpu.VMEM((6, ELEMENTS, 128), F32),
            pltpu.VMEM((32, 128), F32),
            pltpu.VMEM((3, 8, COLS), F32),
            pltpu.VMEM((sizes[0] - 1, 8, COLS), F32),
            pltpu.VMEM((sizes[1] - 1, 8, COLS), F32),
            pltpu.VMEM((sizes[2] - 1, 8, COLS), F32),
            pltpu.SemaphoreType.DMA((3, 4, 4)),
            pltpu.SemaphoreType.DMA((3, 4, 4)),
            pltpu.SemaphoreType.DMA((3, 2)),
            pltpu.SemaphoreType.DMA((3, 2)),
            pltpu.SemaphoreType.DMA((6,)),
            pltpu.SemaphoreType.DMA((6,)),
            pltpu.SemaphoreType.DMA((partners,)),
            pltpu.SemaphoreType.DMA((partners,)),
        ],
        compiler_params=pltpu.CompilerParams(
            collective_id=0, has_side_effects=True, vmem_limit_bytes=20 * MIB
        ),
        name="solver",
    )(diagonals, lmat, forcing)


def recover_kernel(
    vectors, scales, hmat, forcing, traces_hbm, flux_hbm, weights, traces, flux, spread, sems
):
    rows_t, rows_f = 8 * PRESS, 8 * FLUX
    pitch = 5
    first = rows_of((8, COLS)) < 4

    def copies(n):
        slot = n % 2
        return [
            pltpu.make_async_copy(
                traces.at[slot], traces_hbm.at[pl.ds(n * rows_t, rows_t)], sems.at[slot, 0]
            ),
            pltpu.make_async_copy(flux.at[slot], flux_hbm.at[pl.ds(n * rows_f, rows_f)], sems.at[slot, 1]),
        ]

    for n in range(8):
        slot = n % 2
        if n >= 2:
            for item in copies(n - 2):
                item.wait()
        for u in range(8):
            e = 8 * n + u
            tiles = []
            for tile in range(7):
                place = slice(8 * tile, 8 * tile + 8)
                tiles.append(
                    scales[0:8, :] * vectors[0, e, place, :]
                    + scales[8:16, :] * vectors[1, e, place, :]
                    + scales[16:24, :] * vectors[2, e, place, :]
                )
            start = 108 * (u // 4) + u % 4
            for normal in range(3):
                traces[slot, pl.ds(start + 36 * normal, 8, stride=4), :] = tiles[normal]
                line = start + 36 * normal + 32
                traces[slot, line : line + 1, :] = tiles[6][normal : normal + 1]
            high, low = halves(jnp.concatenate(tiles + [jnp.zeros((8, COLS), F32)], axis=0))
            weights[u, 0:TR, :] = high
            weights[u, TR : 2 * TR, :] = low
            weights[u, 2 * TR : 3 * TR, :] = high
            weights[u, 3 * TR : 3 * TR + PR, :] = forcing[e]
            weights[u, 3 * TR + PR :, :] = forcing[e]
        for u in range(8):
            values = jnp.dot(hmat[8 * n + u], weights[u], preferred_element_type=F32)
            spread[pl.ds(FLUX * pitch * (u // 4) + u % 4, FLUX, stride=pitch), :] = -values[0:FLUX]
        for quad in range(FLUX // 2):
            tiles = []
            for half in range(2):
                at = pitch * (4 * quad + 2 * half)
                tiles.append(jnp.where(first, spread[at : at + 8, :], spread[at + 1 : at + 9, :]))
            flux[slot, 16 * quad : 16 * quad + 16, :] = jnp.concatenate(tiles, axis=0).astype(BF16)
        for item in copies(n):
            item.start()
    for n in (6, 7):
        for item in copies(n):
            item.wait()


def recover(vectors, scales, hmat, forcing):
    vmem, hbm = pl.BlockSpec(memory_space=pltpu.VMEM), pl.BlockSpec(memory_space=pltpu.HBM)
    return pl.pallas_call(
        recover_kernel,
        out_shape=(
            jax.ShapeDtypeStruct((ELEMENTS * PRESS, COLS), F32),
            jax.ShapeDtypeStruct((ELEMENTS * FLUX, COLS), BF16),
        ),
        in_specs=[vmem] * 4,
        out_specs=[hbm] * 2,
        scratch_shapes=[
            pltpu.VMEM((8, 256, COLS), BF16),
            pltpu.VMEM((2, 8 * PRESS, COLS), F32),
            pltpu.VMEM((2, 8 * FLUX, COLS), BF16),
            pltpu.VMEM((5 * 2 * FLUX + 8, COLS), F32),
            pltpu.SemaphoreType.DMA((2, 2)),
        ],
        compiler_params=pltpu.CompilerParams(vmem_limit_bytes=16 * MIB),
        name="recover",
    )(vectors, scales, hmat, forcing)


def body(sizes, sources, geometry, rock_class, permeability, mass_inv, div_map, trace_map, dirichlet):
    interleaved = sources.transpose(0, 1, 3, 2, 4).reshape(ELEMENTS * PRESS, COLS)
    lmat, hmat, forcing, diagonals = element_blocks(
        rock_class.transpose(0, 2, 1), dirichlet.transpose(0, 3, 2, 1), geometry, permeability.T,
        mass_inv, div_map, trace_map, interleaved,
    )
    vectors, scales = solve(sizes, diagonals, lmat, forcing)
    traces, flux = recover(vectors, scales, hmat, forcing)
    return (
        traces.reshape(BX, BY, PRESS, BZ, COLS).transpose(0, 1, 3, 2, 4),
        flux.reshape(BX, BY, FLUX, BZ, COLS).transpose(0, 1, 3, 2, 4),
    )


def solution(mesh):
    sizes = (mesh.shape["gx"], mesh.shape["gy"], mesh.shape["gz"])
    placed = (
        P("gx", "gy", "gz", None, None),
        P("gx", "gy", "gz", None),
        P("gx", "gy", "gz"),
        P(),
        P(),
        P(),
        P(),
        P("gx", "gy", "gz", None),
    )
    return jax.shard_map(
        functools.partial(body, sizes),
        mesh=mesh,
        in_specs=placed,
        out_specs=(P("gx", "gy", "gz", None, None), P("gx", "gy", "gz", None, None)),
        check_vma=False,
    )
```

time: 690 us -> 60.4 us (0.09); the launches traced: 682 us -> 59.9 us
  blocking collectives: 325 us -> 0 us
  other arithmetic: 214 us -> 0 us
  Pallas kernels: 0 us -> 53.1 us
  matrix products: 43.4 us -> 0 us
  local copies, waits for them, and re-layouts: 41.3 us -> 6.12 us
  starting transfers between devices: 33.1 us -> 0 us
  waiting for transfers between devices: 21.7 us -> 0 us
    psum x5 -> x0, blocking collectives: 325 us -> none  [global_sum(): return lax.psum(local_value, ('gx', 'gy', 'gz'))]
    another operation x43 -> x0, other arithmetic: 179 us -> none  [the longest x4 160 us: element_blocks(): factor = jnp.linalg.cholesky(schur)]
    pallas_call x0 -> x3, Pallas kernels: none -> 53.1 us  [the longest x1 35.6 us: solve(): pl.pallas_call(functools.partial(solver_kernel, sizes), out_shape=(jax.Sh...]
    dot_general x11 -> x0, matrix products: 37.4 us -> none  [the longest x3 9.47 us: body(): jnp.einsum('ets,esr->etr', condensed, operate_values, precision=finest)]
    ppermute x27 -> x0, starting transfers between devices: 33.1 us -> none  [passed_along(): return lax.ppermute(value, axis, pairs)]
    ppermute x27 -> x0, waiting for transfers between devices: 21.7 us -> none  [passed_along(): return lax.ppermute(value, axis, pairs)]
    add x7 -> x0, other arithmetic: 13.4 us -> none  [combine(): return tuple((left + weight * right for left, right in zip(first, second)))]
    reduce_sum x5 -> x0, other arithmetic: 11.2 us -> none  [column_inner(): return jnp.sum(first[0] * second[0], axis=(0, 1, 2, 3, 4))]
  transfers between devices with their start and end apart: 27 -> 0, of which waited for: 12 -> 0; matrix products, arithmetic and copies ran while one was open for 4% -> 0% of each run, Pallas kernels for 0% -> 0%
where the time goes in v2:
time: 60.4 us; the launch traced here: 59.9 us
  Pallas kernels  53.1 us (88%)
  local copies, waits for them, and re-layouts  6.12 us (10%)
  between operations  0.66 us (1%)
    pallas_call x1, Pallas kernels, solve(): pl.pallas_call(functools.partial(solver_kernel, sizes), out_shape=(jax.Sh...  35.6 us
    pallas_call x1, Pallas kernels, element_blocks(): pl.pallas_call(blocks_kernel, out_shape=(jax.ShapeDtypeStruct((ELEMENTS,...  12.9 us
    unnamed x16, local copies, waits for them, and re-layouts  6.12 us
    pallas_call x1, Pallas kernels, recover(): pl.pallas_call(recover_kernel, out_shape=(jax.ShapeDtypeStruct((ELEMENTS...  4.65 us

profile of v2, /device:TPU:1, one launch (start us, length us, event | category | flops | bytes accessed | tf_op | source)
XLA Modules:
  0.0 59.9 jit_solution(10777259717208393752)
XLA Ops:
  0.6 0.0 copy-start
  0.6 1.0 %copy-done = bf16[2,8,4,27,128]{4,2,3,1,0:T(4,128)(2,1)S(1)} copy-done((bf16[2,8,4,27,128]{4,2,3,1,0:T(4,128)(2,1)S(1)}, bf16[2,8,4,27,128]{4,2,3,1,0:T(4,128)(2,1)}, u32[]{:S(2)}) %copy-start) | copy-done | bytes 442392
  1.6 0.0 copy-start.1
  1.6 0.8 %copy-done.1 = f32[108,108]{1,0:T(8,128)S(1)} copy-done((f32[108,108]{1,0:T(8,128)S(1)}, f32[108,108]{1,0:T(8,128)}, u32[]{:S(2)}) %copy-start.1) | copy-done | bytes 46680
  2.5 0.0 copy-start.2
  2.5 0.8 %copy-done.2 = f32[2,8,4,108]{3,2,1,0:T(4,128)S(1)} copy-done((f32[2,8,4,108]{3,2,1,0:T(4,128)S(1)}, f32[2,8,4,108]{3,2,1,0:T(4,128)}, u32[]{:S(2)}) %copy-start.2) | copy-done | bytes 27672
  3.2 0.0 copy-start.3
  3.2 0.7 %copy-done.3 = f32[54,108]{1,0:T(8,128)S(1)} copy-done((f32[54,108]{1,0:T(8,128)S(1)}, f32[54,108]{1,0:T(8,128)}, u32[]{:S(2)}) %copy-start.3) | copy-done | bytes 23352
  4.0 0.0 copy-start.4
  4.0 0.7 %copy-done.4 = f32[27,108]{1,0:T(8,128)S(1)} copy-done((f32[27,108]{1,0:T(8,128)S(1)}, f32[27,108]{1,0:T(8,128)}, u32[]{:S(2)}) %copy-start.4) | copy-done | bytes 11688
  4.7 0.0 copy-start.5
  4.7 0.7 %copy-done.5 = s32[2,8,4,3]{1,2,3,0:T(4,128)S(1)} copy-done((s32[2,8,4,3]{1,2,3,0:T(4,128)S(1)}, s32[2,8,4,3]{1,2,3,0:T(4,128)}, u32[]{:S(2)}) %copy-start.5) | copy-done | bytes 792
  5.4 0.0 copy-start.6
  5.4 0.7 %copy-done.6 = s32[2,8,4]{1,2,0:T(4,128)S(1)} copy-done((s32[2,8,4]{1,2,0:T(4,128)S(1)}, s32[2,8,4]{1,2,0:T(4,128)}, u32[]{:S(2)}) %copy-start.6) | copy-done | bytes 280
  6.1 0.0 copy-start.7
  6.1 0.7 %copy-done.7 = f32[16,3]{0,1:T(4,128)S(1)} copy-done((f32[16,3]{0,1:T(4,128)S(1)}, f32[16,3]{0,1:T(4,128)}, u32[]{:S(2)}) %copy-start.7) | copy-done | bytes 216
  6.8 12.9 %blocks.1 = (bf16[64,64,256]{2,1,0:T(8,128)(2,1)S(1)}, bf16[64,112,256]{2,1,0:T(8,128)(2,1)S(1)}, bf16[64,32,128]{2,1,0:T(8,128)(2,1)S(1)}, f32[64,128]{1,0:T(8,128)S(1)}) custom-call(s32[2,4,8]{2,1,0:T(4,128)S(1)} %bitcast.14, s32[2,3,4,8]{3,2,1,0:T(4,128)S(1)} %bitcast.13, f32[2,8,4,108]{3,2,1,0:T(4,128)S(1)} %copy-done.2, f32[3,16]{1,0:T(4,128)S(1)} %bitcast.15, ...), custom_call_target="tpu_custom_call" | custom-call | tf_op jit(solution)/shard_map/blocks/pallas_call | solution.py:252
  19.7 35.6 %solver.1 = (f32[3,64,64,128]{3,2,1,0:T(8,128)S(1)}, f32[24,128]{1,0:T(8,128)S(1)}) custom-call(f32[64,128]{1,0:T(8,128)S(1)} %get-tuple-element.10.diagonals, bf16[64,64,256]{2,1,0:T(8,128)(2,1)S(1)} %get-tuple-element.11.lmat, bf16[64,32,128]{2,1,0:T(8,128)(2,1)S(1)} %get-tuple-element.12.forcing), custom_call_target="tpu_custom_call" | custom-call | tf_op jit(solution)/shard_map/solver/pallas_call | solution.py:582
  55.3 4.7 %recover.1 = (f32[1728,128]{1,0:T(8,128)}, bf16[6912,128]{1,0:T(8,128)(2,1)}) custom-call(f32[3,64,64,128]{3,2,1,0:T(8,128)S(1)} %get-tuple-element.13.vectors, f32[24,128]{1,0:T(8,128)S(1)} %get-tuple-element.14.scales, bf16[64,112,256]{2,1,0:T(8,128)(2,1)S(1)} %get-tuple-element.15.hmat, bf16[64,32,128]{2,1,0:T(8,128)(2,1)S(1)} %get-tuple-element.12.forcing), custom_call_target="tpu_custom_call" | custom-call | tf_op jit(solution)/shard_map/recover/pallas_call | solution.py:678
Async XLA Ops:
  0.6 1.0 %copy-start = (bf16[2,8,4,27,128]{4,2,3,1,0:T(4,128)(2,1)S(1)}, bf16[2,8,4,27,128]{4,2,3,1,0:T(4,128)(2,1)}, u32[]{:S(2)}) copy-start(bf16[2,8,4,27,128]{4,2,3,1,0:T(4,128)(2,1)} %param.8) | copy-start | bytes 1327108
  1.6 0.8 %copy-start.1 = (f32[108,108]{1,0:T(8,128)S(1)}, f32[108,108]{1,0:T(8,128)}, u32[]{:S(2)}) copy-start(f32[108,108]{1,0:T(8,128)} %mass_hbm.1) | copy-start | bytes 139972
  2.5 0.8 %copy-start.2 = (f32[2,8,4,108]{3,2,1,0:T(4,128)S(1)}, f32[2,8,4,108]{3,2,1,0:T(4,128)}, u32[]{:S(2)}) copy-start(f32[2,8,4,108]{3,2,1,0:T(4,128)} %geometry_hbm.1) | copy-start | bytes 82948
  3.2 0.7 %copy-start.3 = (f32[54,108]{1,0:T(8,128)S(1)}, f32[54,108]{1,0:T(8,128)}, u32[]{:S(2)}) copy-start(f32[54,108]{1,0:T(8,128)} %trace_hbm.1) | copy-start | bytes 69988
  4.0 0.7 %copy-start.4 = (f32[27,108]{1,0:T(8,128)S(1)}, f32[27,108]{1,0:T(8,128)}, u32[]{:S(2)}) copy-start(f32[27,108]{1,0:T(8,128)} %div_hbm.1) | copy-start | bytes 34996
  4.7 0.7 %copy-start.5 = (s32[2,8,4,3]{1,2,3,0:T(4,128)S(1)}, s32[2,8,4,3]{1,2,3,0:T(4,128)}, u32[]{:S(2)}) copy-start(s32[2,8,4,3]{1,2,3,0:T(4,128)} %param.15) | copy-start | bytes 2308
  5.4 0.7 %copy-start.6 = (s32[2,8,4]{1,2,0:T(4,128)S(1)}, s32[2,8,4]{1,2,0:T(4,128)}, u32[]{:S(2)}) copy-start(s32[2,8,4]{1,2,0:T(4,128)} %param.10) | copy-start | bytes 772
  6.1 0.7 %copy-start.7 = (f32[16,3]{0,1:T(4,128)S(1)}, f32[16,3]{0,1:T(4,128)}, u32[]{:S(2)}) copy-start(f32[16,3]{0,1:T(4,128)} %param.11) | copy-start | bytes 580

commit v3 on v2

--- a/solution.py
+++ b/solution.py
@@ -33,6 +33,8 @@
 
 BATCH = 16
 
+GRANT = 62 * MIB
+
 
 def lanes_of(shape):
     return lax.broadcasted_iota(jnp.int32, shape, len(shape) - 1)
@@ -47,13 +49,21 @@
     return high, (value - high.astype(F32)).astype(BF16)
 
 
-def blocks_kernel(
-    rock, dirichlet, geometry_hbm, permeability_hbm, mass_hbm, div_hbm, trace_hbm, sources_hbm,
-    lmat, hmat, forcing, diagonals,
-    geometry, permeability, mass_in, div_map, trace_map, sources,
-    joined, joined_t, padded, scale_t, left_mass, left_joined,
-    highs, lows, press, inverse, table, spread, columns, first, second, solved_in, right, sems,
-):
+def packed_pair(value):
+    first, second = value[:, 0:128], value[:, 128:256]
+    lane = lanes_of(second.shape)
+    kept = (lane >= TR) & (lane < TR + PR)
+    return first, jnp.where(kept, second, second - second.astype(BF16).astype(F32)).astype(BF16)
+
+
+def local_blocks(arguments, results, scratch, sems):
+    sources_hbm, geometry_hbm, rock_hbm, permeability_hbm, mass_hbm, div_hbm, trace_hbm, dirichlet_hbm = arguments
+    diagonals, highs, lows, duals, right = results
+    (
+        geometry, rock, permeability, mass_in, div_map, trace_map, dirichlet, sources,
+        joined, joined_t, padded, scale_t, left_mass, left_joined,
+        press, inverse, table, spread, columns, first, second, solved_in, work,
+    ) = scratch
     loads = [
         pltpu.make_async_copy(source, target, sems.at[n])
         for n, (source, target) in enumerate(
@@ -62,7 +72,9 @@
                 (div_hbm, div_map),
                 (mass_hbm, mass_in),
                 (permeability_hbm, permeability),
+                (rock_hbm, rock),
                 (geometry_hbm, geometry),
+                (dirichlet_hbm, dirichlet),
                 (sources_hbm, sources),
             )
         )
@@ -100,6 +112,7 @@
     )
     padded[...] = jnp.zeros_like(padded)
     loads[4].wait()
+    loads[5].wait()
     for e in range(ELEMENTS):
         i, j, k = e // 32, (e // 4) % 8, e % 4
         row = table[pl.ds(rock[i, k, j], 1), :][:, 0:FLUX]
@@ -111,6 +124,8 @@
         for part in range(3):
             first[pair, 128 * part + FR : 128 * part + 128, :] = no_rows
             second[pair, 128 * part + FR : 128 * part + 128, :] = no_rows
+
+    on_diagonal = lanes_of((TR, 128)) == rows_of((TR, 128))
 
     @pl.loop(0, ELEMENTS // BATCH)
     def build(step):
@@ -143,37 +158,38 @@
                 cut = slice(128 * n, 128 * n + 128)
                 highs[e, 0:TR, :] = high[:, cut]
                 lows[e, 0:TR, :] = low[:, cut]
+                diagonals[pl.ds(e, 1), :] = jnp.sum(
+                    jnp.where(on_diagonal, coupled[0:TR, cut], 0.0), axis=0, keepdims=True
+                )
                 press[pl.ds(pl.multiple_of(e * PR, PR), PR), :] = coupled[TR:, cut]
 
     low_half = lanes_of((PR, 128)) < 64
     row_of = rows_of((PR, 128))
 
-    def invert(work):
-        for pair in range(14):
-            rows = [press[pl.ds(2 * pair + n, ELEMENTS, stride=PR), :] for n in range(2)]
-            work[pair] = jnp.transpose(jnp.concatenate(rows, axis=0))[TR : TR + PR, :]
-
-        for k in range(PRESS):
-            owner, ahead = k // 2, (k + 1) // 2 % 14
-            mine = row_of == k
-            held = low_half if k % 2 == 0 else jnp.logical_not(low_half)
-            source = work[owner]
-            source = jnp.where(held, source, pltpu.roll(source, 64, 1))
-            row = jnp.where(mine, 1.0, source) * (1.0 / source[k : k + 1, :])
-            for pair in [ahead] + [p for p in range(14) if p != ahead]:
-                value = work[pair]
-                value = jnp.where(mine, 0.0, value) - value[k : k + 1, :] * row
-                work[pair] = jnp.where(held, row, value) if pair == owner else value
-
-        for pair in range(14):
-            placed = jnp.concatenate(
-                [work[pair], jnp.zeros((PR, 128), F32), work[pair], work[pair]], axis=0
-            )
-            turned = jnp.transpose(placed)
-            inverse[pl.ds(2 * pair, ELEMENTS, stride=PR), :] = turned[0:ELEMENTS]
-            inverse[pl.ds(2 * pair + 1, ELEMENTS, stride=PR), :] = turned[ELEMENTS:]
-
-    pl.run_scoped(invert, pltpu.VMEM((14, PR, 128), F32))
+    for pair in range(14):
+        rows = [press[pl.ds(2 * pair + n, ELEMENTS, stride=PR), :] for n in range(2)]
+        work[pair] = jnp.transpose(jnp.concatenate(rows, axis=0))[TR : TR + PR, :]
+
+    for k in range(PRESS):
+        owner, ahead = k // 2, (k + 1) // 2 % 14
+        mine = row_of == k
+        held = low_half if k % 2 == 0 else jnp.logical_not(low_half)
+        source = work[owner]
+        source = jnp.where(held, source, pltpu.roll(source, 64, 1))
+        row = jnp.where(mine, 1.0, source) * (1.0 / source[k : k + 1, :])
+        for pair in [ahead] + [p for p in range(14) if p != ahead]:
+            value = work[pair]
+            value = jnp.where(mine, 0.0, value) - value[k : k + 1, :] * row
+            work[pair] = jnp.where(held, row, value) if pair == owner else value
+
+    for pair in range(14):
+        placed = jnp.concatenate(
+            [work[pair], jnp.zeros((PR, 128), F32), work[pair], work[pair]], axis=0
+        )
+        turned = jnp.transpose(placed)
+        inverse[pl.ds(2 * pair, ELEMENTS, stride=PR), :] = turned[0:ELEMENTS]
+        inverse[pl.ds(2 * pair + 1, ELEMENTS, stride=PR), :] = turned[ELEMENTS:]
+
 
     lane = lanes_of((TR, 256))
     unit = jnp.where((jnp.bitwise_and(lane, 63) == rows_of((TR, 256))) & (lane < 192), 1.0, 0.0)
@@ -184,11 +200,7 @@
         right[u, 128:192, :] = unit
         right[u, 224:256, :] = jnp.zeros((PR, 256), BF16)
     lane = lanes_of((PR, 128))
-    lane_t = lanes_of((TR, 128))
-    on_diagonal = lane_t == rows_of((TR, 128))
     line = lanes_of((1, 128))
-    lane_f = lanes_of((AR, 128))
-    kept_high = (lane_f >= TR) & (lane_f < TR + PR)
     x_lanes = (line < 8) | (line == 48)
     y_lanes = ((line >= 8) & (line < 16)) | (line == 49)
     z_lanes = ((line >= 16) & (line < 24)) | (line == 50)
@@ -206,27 +218,15 @@
             inv = inverse[pl.ds(pl.multiple_of(e * PR, PR), PR), :]
             left = jnp.where(lane < TR + PR, inv, inv - inv.astype(BF16).astype(F32)).astype(BF16)
             solved = jnp.dot(left, solved_in[u], preferred_element_type=F32)
+            taken = press[pl.ds(pl.multiple_of(e * PR, PR), PR), :] * solved
+            diagonals[pl.ds(e, 1), :] = diagonals[pl.ds(e, 1), :] - jnp.sum(taken, axis=0, keepdims=True)
             for part, other in enumerate((pltpu.roll(solved, TR, 1), inv)):
                 high, low = halves(-jnp.where(lane < TR, solved, other))
                 cut = slice(128 * part, 128 * part + 128)
-                right[u, 64:96, cut] = high
-                right[u, 96:128, cut] = low
-                right[u, 192:224, cut] = high
-        for u in range(BATCH):
-            e = step * BATCH + u
-            left = jnp.concatenate([highs[e], lows[e]], axis=1)
-            result = jnp.dot(left, right[u], preferred_element_type=F32)
-            both, rest = result[:, 0:128], result[:, 128:256]
-            diagonals[pl.ds(e, 1), :] = jnp.sum(
-                jnp.where(on_diagonal, both[0:TR], 0.0), axis=0, keepdims=True
-            )
-            both = both.astype(BF16)
-            rest = jnp.where(kept_high, rest, rest - rest.astype(BF16).astype(F32)).astype(BF16)
-            lmat[e, :, 0:128] = both[0:TR]
-            lmat[e, :, 128:256] = rest[0:TR]
-            hmat[e, :, 0:128] = both[TR:]
-            hmat[e, :, 128:256] = rest[TR:]
-
+                duals[e, 0:PR, cut] = high
+                duals[e, PR:TR, cut] = low
+
+    loads[6].wait()
     for e in range(ELEMENTS):
         i, j, k = e // 32, (e // 4) % 8, e % 4
         lift = [dirichlet[i, normal, k, j].astype(F32) * BLOCKED for normal in range(3)]
@@ -234,7 +234,10 @@
             x_lanes, lift[0], jnp.where(y_lanes, lift[1], jnp.where(z_lanes, lift[2], 0.0))
         )
 
-    loads[5].wait()
+    return loads[7]
+
+
+def spread_forcing(sources, spread, forcing):
     for part in range(4):
         spread[...] = sources[432 * part : 432 * part + 432, :].astype(F32)
         for jj in range(4):
@@ -243,51 +246,6 @@
                 values = spread[pl.ds(108 * jj + k, PRESS, stride=4), :]
                 values = jnp.concatenate([values, jnp.zeros((PR - PRESS, COLS), F32)], axis=0)
                 forcing[e] = values.astype(BF16)
-
-
-def element_blocks(rock_class, dirichlet, geometry, permeability, mass_inv, div_map, trace_map, sources):
-    smem, hbm, vmem = [
-        pl.BlockSpec(memory_space=space) for space in (pltpu.SMEM, pltpu.HBM, pltpu.VMEM)
-    ]
-    return pl.pallas_call(
-        blocks_kernel,
-        out_shape=(
-            jax.ShapeDtypeStruct((ELEMENTS, TR, 256), BF16),
-            jax.ShapeDtypeStruct((ELEMENTS, FR, 256), BF16),
-            jax.ShapeDtypeStruct((ELEMENTS, PR, COLS), BF16),
-            jax.ShapeDtypeStruct((ELEMENTS, 128), F32),
-        ),
-        in_specs=[smem] * 2 + [hbm] * 6,
-        out_specs=[vmem] * 4,
-        scratch_shapes=[
-            pltpu.VMEM(geometry.shape, F32),
-            pltpu.VMEM(permeability.shape, F32),
-            pltpu.VMEM(mass_inv.shape, F32),
-            pltpu.VMEM(div_map.shape, F32),
-            pltpu.VMEM(trace_map.shape, F32),
-            pltpu.VMEM(sources.shape, BF16),
-            pltpu.VMEM((128, 128), F32),
-            pltpu.VMEM((128, 128), F32),
-            pltpu.VMEM((128, 128), F32),
-            pltpu.VMEM((128, 128), F32),
-            pltpu.VMEM((FR, 384), BF16),
-            pltpu.VMEM((TR + PR, 384), BF16),
-            pltpu.VMEM((ELEMENTS, AR, 128), BF16),
-            pltpu.VMEM((ELEMENTS, AR, 128), BF16),
-            pltpu.VMEM((ELEMENTS * PR, 128), F32),
-            pltpu.VMEM((ELEMENTS * PR, 128), F32),
-            pltpu.VMEM((16, 128), F32),
-            pltpu.VMEM((432, 128), F32),
-            pltpu.VMEM((BATCH // 2, FR, 256), F32),
-            pltpu.VMEM((BATCH // 2, 384, 256), BF16),
-            pltpu.VMEM((BATCH // 2, 384, 256), BF16),
-            pltpu.VMEM((BATCH, 128, 128), BF16),
-            pltpu.VMEM((BATCH, 256, 256), BF16),
-            pltpu.SemaphoreType.DMA((6,)),
-        ],
-        compiler_params=pltpu.CompilerParams(vmem_limit_bytes=28 * MIB),
-        name="blocks",
-    )(rock_class, dirichlet, geometry, permeability, mass_inv, div_map, trace_map, sources)
 
 
 def facet_rows(g, i, jj, k):
@@ -327,11 +285,14 @@
     return i * 32 + g * 8 + jj * 4 + k
 
 
-def solver_kernel(
-    sizes, diagonals, lmat, forcing, vectors, scales,
-    low, up, inverse, fields, weights, near, turned, mine, parts_x, parts_y, parts_z,
-    send, recv, send_y, recv_y, send_d, recv_d, send_sum, recv_sum,
-):
+def solver_kernel(sizes, *refs):
+    arguments, (lam_hbm, hmat_hbm, forcing_hbm) = refs[:8], refs[8:11]
+    (
+        lmat, hmat, forcing, diagonals, highs, lows, duals, right,
+        low, up, inverse, fields, vectors, weights, lam, near, turned, mine, parts_a, parts_b,
+        load_sems, out_sems, send, recv, send_y, recv_y, send_d, recv_d, send_sum, recv_sum,
+    ) = refs[11:41]
+    local_scratch = refs[41:]
     nx, ny, nz = sizes
     ix, iy, iz = lax.axis_index("gx"), lax.axis_index("gy"), lax.axis_index("gz")
 
@@ -344,9 +305,14 @@
     def at_z(step):
         return (ix, iy, lax.rem(iz + step + nz, nz))
 
-    partners = (
-        [at_x(s) for s in range(1, nx)] + [at_y(s) for s in range(1, ny)] + [at_z(s) for s in range(1, nz)]
-    )
+    def at_xy(a, b):
+        return (lax.rem(ix + a, nx), lax.rem(iy + b, ny), iz)
+
+    rings = [
+        [at_xy(a, b) for a in range(nx) for b in range(ny) if (a, b) != (0, 0)],
+        [at_z(s) for s in range(1, nz)],
+    ]
+    partners = rings[0] + rings[1]
     barrier = pltpu.get_barrier_semaphore()
     for partner in partners:
         pl.semaphore_signal(barrier, inc=1, device_id=partner, device_id_type=MESH)
@@ -395,6 +361,9 @@
             return field_copy(low, stage, first, last, GROUP, send_y.at[stage, 0], recv_y.at[stage, 0], at_y(-1))
         return field_copy(up, stage, last, first, GROUP, send_y.at[stage, 1], recv_y.at[stage, 1], at_y(1))
 
+    sources_load = local_blocks(
+        arguments, (diagonals, highs, lows, duals, right), local_scratch, load_sems
+    )
     pl.semaphore_wait(barrier, len(partners))
 
     half = ELEMENTS // 2
@@ -420,13 +389,31 @@
             def _():
                 copy_y(stage, side).start()
 
+    sources_load.wait()
+    spread_forcing(local_scratch[7], local_scratch[17], forcing)
+    out_copies = [pltpu.make_async_copy(forcing, forcing_hbm, out_sems.at[0])]
+    out_copies[0].start()
+
+    def fill_right(u, e):
+        right[u, 64:96, :] = duals[e, 0:PR, :]
+        right[u, 96:128, :] = duals[e, PR:TR, :]
+        right[u, 192:224, :] = duals[e, 0:PR, :]
+
     @pl.loop(0, 4)
     def start(n):
         g = order(n)
+        for u, (i, jj, k) in enumerate(EACH):
+            fill_right(u, element_index(g, i, jj, k))
+        for u, (i, jj, k) in enumerate(EACH):
+            e = element_index(g, i, jj, k)
+            left = jnp.concatenate([highs[e, 0:TR, :], lows[e, 0:TR, :]], axis=1)
+            both, rest = packed_pair(jnp.dot(left, right[u], preferred_element_type=F32))
+            lmat[e, :, 0:128] = both.astype(BF16)
+            lmat[e, :, 128:256] = rest
         for i, jj, k in EACH:
             e = element_index(g, i, jj, k)
-            right = jnp.concatenate([jnp.zeros((TR, COLS), BF16), forcing[e], forcing[e]], axis=0)
-            values = -jnp.dot(lmat[e, :, 128:256], right, preferred_element_type=F32)
+            given = jnp.concatenate([jnp.zeros((TR, COLS), BF16), forcing[e], forcing[e]], axis=0)
+            values = -jnp.dot(lmat[e, :, 128:256], given, preferred_element_type=F32)
             scatter(values, low.at[0], up.at[0], facet_rows(g, i, jj, k))
         send_chunk(0, n)
 
@@ -536,19 +523,33 @@
         line = jnp.broadcast_to(jnp.sum(moment, axis=0, keepdims=True), (8, COLS))
         tile = jnp.where(sublane == which, line, tile)
 
-    offset = 0
-    for stage, (count, at, parts) in enumerate(((nx, at_x, parts_x), (ny, at_y, parts_y), (nz, at_z, parts_z))):
+    def recovery(batch):
+        for u in range(BATCH):
+            e = batch * BATCH + u
+            fill_right(u, e)
+        for u in range(BATCH):
+            e = batch * BATCH + u
+            left = jnp.concatenate([highs[e, TR:AR, :], lows[e, TR:AR, :]], axis=1)
+            both, rest = packed_pair(jnp.dot(left, right[u], preferred_element_type=F32))
+            hmat[e, :, 0:128] = both.astype(BF16)
+            hmat[e, :, 128:256] = rest
+
+    batches = ELEMENTS // BATCH
+    for stage, (ring, parts) in enumerate(zip(rings, (parts_a, parts_b))):
         mine[stage] = tile
-        copies = [
-            remote(mine.at[stage], parts.at[s - 1], send_sum.at[offset + s - 1], recv_sum.at[offset + s - 1], at(s))
-            for s in range(1, count)
-        ]
-        for item in copies:
-            item.start()
-        for s, item in enumerate(copies):
-            item.wait()
-            tile = tile + parts[s]
-        offset += count - 1
+        for n, partner in enumerate(ring):
+            remote(mine.at[stage], parts.at[n], send_sum.at[stage], recv_sum.at[stage], partner).start()
+        span = (0, batches // 2) if stage == 0 else (batches // 2, batches)
+        pl.loop(*span)(recovery)
+        place = pl.ds(span[0] * BATCH, (span[1] - span[0]) * BATCH)
+        out_copies.append(pltpu.make_async_copy(hmat.at[place], hmat_hbm.at[place], out_sems.at[1 + stage]))
+        out_copies[-1].start()
+        pltpu.make_async_copy(parts, parts, recv_sum.at[stage]).wait()
+        terms = [tile] + [parts[n] for n in range(len(ring))]
+        while len(terms) > 1:
+            terms = [sum(terms[n : n + 2][1:], terms[n]) for n in range(0, len(terms), 2)]
+        tile = terms[0]
+        pltpu.make_async_copy(parts, parts, send_sum.at[stage]).wait()
 
     b0, g00, g11, g01, g22, g12 = [tile[n : n + 1] for n in range(6)]
     b1 = g00 - b0
@@ -563,8 +564,20 @@
     c2 = jnp.where(k22 > 2e-6 * g22, (d2 - m * d1) / k22, 0.0)
     c1 = jnp.where(sound, (d1 - h12 * c2) / h11, 0.0)
     c0 = (b0 - g01 * c1 - g02 * c2) / g00
-    for n, c in enumerate((c0, c1, c2)):
-        scales[8 * n : 8 * n + 8, :] = jnp.broadcast_to(c, (8, COLS))
+    c0, c1, c2 = [jnp.broadcast_to(c, (8, COLS)) for c in (c0, c1, c2)]
+
+    for part in range(2):
+        @pl.loop(32 * part, 32 * part + 32)
+        def combine(e):
+            for tile in range(7):
+                place = slice(8 * tile, 8 * tile + 8)
+                lam[e, place, :] = (
+                    c0 * vectors[0, e, place, :] + c1 * vectors[1, e, place, :] + c2 * vectors[2, e, place, :]
+                )
+
+        place = pl.ds(32 * part, 32)
+        out_copies.append(pltpu.make_async_copy(lam.at[place], lam_hbm.at[place], out_sems.at[3 + part]))
+        out_copies[-1].start()
 
     @pl.loop(0, 4)
     def drain(g):
@@ -577,132 +590,173 @@
             copy_y(stage, side).wait_send()
 
 
-def solve(sizes, diagonals, lmat, forcing):
-    partners = sum(sizes) - 3
+    for item in out_copies:
+        item.wait()
+
+
+def solve(sizes, *arguments):
+    hbm = pl.BlockSpec(memory_space=pltpu.HBM)
+    _, geometry, rock, permeability, mass_inv, div_map, trace_map, dirichlet = arguments
+    dma = pltpu.SemaphoreType.DMA
     return pl.pallas_call(
         functools.partial(solver_kernel, sizes),
         out_shape=(
-            jax.ShapeDtypeStruct((3, ELEMENTS, TR, COLS), F32),
-            jax.ShapeDtypeStruct((24, COLS), F32),
+            jax.ShapeDtypeStruct((ELEMENTS, 56, COLS), F32),
+            jax.ShapeDtypeStruct((ELEMENTS, FR, 256), BF16),
+            jax.ShapeDtypeStruct((ELEMENTS, PR, COLS), BF16),
         ),
-        in_specs=[pl.BlockSpec(memory_space=pltpu.VMEM)] * 3,
-        out_specs=[pl.BlockSpec(memory_space=pltpu.VMEM)] * 2,
+        in_specs=[hbm] * 8,
+        out_specs=[hbm] * 3,
         scratch_shapes=[
+            pltpu.VMEM((ELEMENTS, TR, 256), BF16),
+            pltpu.VMEM((ELEMENTS, FR, 256), BF16),
+            pltpu.VMEM((ELEMENTS, PR, COLS), BF16),
+            pltpu.VMEM((ELEMENTS, 128), F32),
+            pltpu.VMEM((ELEMENTS, AR, 128), BF16),
+            pltpu.VMEM((ELEMENTS, AR, 128), BF16),
+            pltpu.VMEM((ELEMENTS, TR, 256), BF16),
+            pltpu.VMEM((BATCH, 256, 256), BF16),
             pltpu.VMEM((3, FIELD, COLS), F32),
             pltpu.VMEM((3, FIELD, COLS), F32),
             pltpu.VMEM((FIELD, COLS), F32),
             pltpu.VMEM((3, FIELD, COLS), F32),
+            pltpu.VMEM((3, ELEMENTS, TR, COLS), F32),
             pltpu.VMEM((len(EACH), 256, COLS), BF16),
+            pltpu.VMEM((ELEMENTS, 56, COLS), F32),
             pltpu.VMEM((6, ELEMENTS, 128), F32),
             pltpu.VMEM((32, 128), F32),
-            pltpu.VMEM((3, 8, COLS), F32),
-            pltpu.VMEM((sizes[0] - 1, 8, COLS), F32),
-            pltpu.VMEM((sizes[1] - 1, 8, COLS), F32),
+            pltpu.VMEM((2, 8, COLS), F32),
+            pltpu.VMEM((sizes[0] * sizes[1] - 1, 8, COLS), F32),
             pltpu.VMEM((sizes[2] - 1, 8, COLS), F32),
-            pltpu.SemaphoreType.DMA((3, 4, 4)),
-            pltpu.SemaphoreType.DMA((3, 4, 4)),
-            pltpu.SemaphoreType.DMA((3, 2)),
-            pltpu.SemaphoreType.DMA((3, 2)),
-            pltpu.SemaphoreType.DMA((6,)),
-            pltpu.SemaphoreType.DMA((6,)),
-            pltpu.SemaphoreType.DMA((partners,)),
-            pltpu.SemaphoreType.DMA((partners,)),
+            dma((8,)), dma((5,)),
+            dma((3, 4, 4)), dma((3, 4, 4)), dma((3, 2)), dma((3, 2)), dma((6,)), dma((6,)), dma((2,)), dma((2,)),
+            pltpu.VMEM(geometry.shape, F32),
+            pltpu.SMEM(rock.shape, jnp.int32),
+            pltpu.VMEM(permeability.shape, F32),
+            pltpu.VMEM(mass_inv.shape, F32),
+            pltpu.VMEM(div_map.shape, F32),
+            pltpu.VMEM(trace_map.shape, F32),
+            pltpu.SMEM(dirichlet.shape, jnp.int32),
+            pltpu.VMEM((ELEMENTS * PRESS, COLS), BF16),
+            pltpu.VMEM((128, 128), F32),
+            pltpu.VMEM((128, 128), F32),
+            pltpu.VMEM((128, 128), F32),
+            pltpu.VMEM((128, 128), F32),
+            pltpu.VMEM((FR, 384), BF16),
+            pltpu.VMEM((TR + PR, 384), BF16),
+            pltpu.VMEM((ELEMENTS * PR, 128), F32),
+            pltpu.VMEM((ELEMENTS * PR, 128), F32),
+            pltpu.VMEM((16, 128), F32),
+            pltpu.VMEM((432, 128), F32),
+            pltpu.VMEM((BATCH // 2, FR, 256), F32),
+            pltpu.VMEM((BATCH // 2, 384, 256), BF16),
+            pltpu.VMEM((BATCH // 2, 384, 256), BF16),
+            pltpu.VMEM((BATCH, 128, 128), BF16),
+            pltpu.VMEM((14, PR, 128), F32),
         ],
         compiler_params=pltpu.CompilerParams(
-            collective_id=0, has_side_effects=True, vmem_limit_bytes=20 * MIB
+            collective_id=0, has_side_effects=True, vmem_limit_bytes=GRANT
         ),
         name="solver",
-    )(diagonals, lmat, forcing)
-
-
-def recover_kernel(
-    vectors, scales, hmat, forcing, traces_hbm, flux_hbm, weights, traces, flux, spread, sems
-):
-    rows_t, rows_f = 8 * PRESS, 8 * FLUX
+    )(*arguments)
+
+
+def recover_kernel(lam_hbm, hmat_hbm, forcing_hbm, traces_hbm, flux_hbm,
+                   lam, hmat, forcing, traces, flux, weights, spread, load_sems, out_sems):
     pitch = 5
     first = rows_of((8, COLS)) < 4
-
-    def copies(n):
-        slot = n % 2
+    parts = ELEMENTS // BATCH
+    rows_t, rows_f = BATCH * PRESS, BATCH * FLUX
+
+    def loads(n):
+        place = pl.ds(n * BATCH, BATCH)
+        return [
+            pltpu.make_async_copy(source.at[place], target.at[place], load_sems.at[n, which])
+            for which, (source, target) in enumerate(
+                ((lam_hbm, lam), (hmat_hbm, hmat), (forcing_hbm, forcing))
+            )
+        ]
+
+    def stores(n):
         return [
             pltpu.make_async_copy(
-                traces.at[slot], traces_hbm.at[pl.ds(n * rows_t, rows_t)], sems.at[slot, 0]
-            ),
-            pltpu.make_async_copy(flux.at[slot], flux_hbm.at[pl.ds(n * rows_f, rows_f)], sems.at[slot, 1]),
+                source.at[pl.ds(n * rows, rows)], target.at[pl.ds(n * rows, rows)], out_sems.at[n, which]
+            )
+            for which, (source, target, rows) in enumerate(
+                ((traces, traces_hbm, rows_t), (flux, flux_hbm, rows_f))
+            )
         ]
 
-    for n in range(8):
-        slot = n % 2
-        if n >= 2:
-            for item in copies(n - 2):
-                item.wait()
-        for u in range(8):
-            e = 8 * n + u
-            tiles = []
-            for tile in range(7):
-                place = slice(8 * tile, 8 * tile + 8)
-                tiles.append(
-                    scales[0:8, :] * vectors[0, e, place, :]
-                    + scales[8:16, :] * vectors[1, e, place, :]
-                    + scales[16:24, :] * vectors[2, e, place, :]
-                )
-            start = 108 * (u // 4) + u % 4
+    for n in range(parts):
+        for item in loads(n):
+            item.start()
+
+    @pl.loop(0, parts)
+    def part(n):
+        for item in loads(n):
+            item.wait()
+        for u in range(BATCH):
+            e = n * BATCH + u
+            tiles = [lam[e, 8 * tile : 8 * tile + 8, :] for tile in range(7)]
+            start = n * rows_t + 108 * (u // 4) + u % 4
             for normal in range(3):
-                traces[slot, pl.ds(start + 36 * normal, 8, stride=4), :] = tiles[normal]
-                line = start + 36 * normal + 32
-                traces[slot, line : line + 1, :] = tiles[6][normal : normal + 1]
+                traces[pl.ds(start + 36 * normal, 8, stride=4), :] = tiles[normal]
+                traces[pl.ds(start + 36 * normal + 32, 1), :] = tiles[6][normal : normal + 1]
             high, low = halves(jnp.concatenate(tiles + [jnp.zeros((8, COLS), F32)], axis=0))
             weights[u, 0:TR, :] = high
             weights[u, TR : 2 * TR, :] = low
             weights[u, 2 * TR : 3 * TR, :] = high
             weights[u, 3 * TR : 3 * TR + PR, :] = forcing[e]
             weights[u, 3 * TR + PR :, :] = forcing[e]
-        for u in range(8):
-            values = jnp.dot(hmat[8 * n + u], weights[u], preferred_element_type=F32)
+        for u in range(BATCH):
+            values = jnp.dot(hmat[n * BATCH + u], weights[u], preferred_element_type=F32)
             spread[pl.ds(FLUX * pitch * (u // 4) + u % 4, FLUX, stride=pitch), :] = -values[0:FLUX]
-        for quad in range(FLUX // 2):
+        for quad in range(BATCH * FLUX // 16):
             tiles = []
             for half in range(2):
                 at = pitch * (4 * quad + 2 * half)
                 tiles.append(jnp.where(first, spread[at : at + 8, :], spread[at + 1 : at + 9, :]))
-            flux[slot, 16 * quad : 16 * quad + 16, :] = jnp.concatenate(tiles, axis=0).astype(BF16)
-        for item in copies(n):
+            place = pl.ds(pl.multiple_of(n * rows_f + 16 * quad, 16), 16)
+            flux[place, :] = jnp.concatenate(tiles, axis=0).astype(BF16)
+        for item in stores(n):
             item.start()
-    for n in (6, 7):
-        for item in copies(n):
+
+    for n in range(parts):
+        for item in stores(n):
             item.wait()
 
 
-def recover(vectors, scales, hmat, forcing):
-    vmem, hbm = pl.BlockSpec(memory_space=pltpu.VMEM), pl.BlockSpec(memory_space=pltpu.HBM)
+def recover(lam, hmat, forcing):
+    hbm = pl.BlockSpec(memory_space=pltpu.HBM)
+    out_shape = (
+        jax.ShapeDtypeStruct((ELEMENTS * PRESS, COLS), F32),
+        jax.ShapeDtypeStruct((ELEMENTS * FLUX, COLS), BF16),
+    )
     return pl.pallas_call(
         recover_kernel,
-        out_shape=(
-            jax.ShapeDtypeStruct((ELEMENTS * PRESS, COLS), F32),
-            jax.ShapeDtypeStruct((ELEMENTS * FLUX, COLS), BF16),
-        ),
-        in_specs=[vmem] * 4,
+        out_shape=out_shape,
+        in_specs=[hbm] * 3,
         out_specs=[hbm] * 2,
         scratch_shapes=[
-            pltpu.VMEM((8, 256, COLS), BF16),
-            pltpu.VMEM((2, 8 * PRESS, COLS), F32),
-            pltpu.VMEM((2, 8 * FLUX, COLS), BF16),
-            pltpu.VMEM((5 * 2 * FLUX + 8, COLS), F32),
-            pltpu.SemaphoreType.DMA((2, 2)),
+            pltpu.VMEM(item.shape, item.dtype) for item in (lam, hmat, forcing) + out_shape
+        ] + [
+            pltpu.VMEM((BATCH, 256, COLS), BF16),
+            pltpu.VMEM((5 * BATCH * FLUX // 4 + 8, COLS), F32),
+            pltpu.SemaphoreType.DMA((ELEMENTS // BATCH, 3)),
+            pltpu.SemaphoreType.DMA((ELEMENTS // BATCH, 2)),
         ],
-        compiler_params=pltpu.CompilerParams(vmem_limit_bytes=16 * MIB),
+        compiler_params=pltpu.CompilerParams(vmem_limit_bytes=GRANT),
         name="recover",
-    )(vectors, scales, hmat, forcing)
+    )(lam, hmat, forcing)
 
 
 def body(sizes, sources, geometry, rock_class, permeability, mass_inv, div_map, trace_map, dirichlet):
     interleaved = sources.transpose(0, 1, 3, 2, 4).reshape(ELEMENTS * PRESS, COLS)
-    lmat, hmat, forcing, diagonals = element_blocks(
-        rock_class.transpose(0, 2, 1), dirichlet.transpose(0, 3, 2, 1), geometry, permeability.T,
-        mass_inv, div_map, trace_map, interleaved,
+    lam, hmat, forcing = solve(
+        sizes, interleaved, geometry, rock_class.transpose(0, 2, 1), permeability.T,
+        mass_inv, div_map, trace_map, dirichlet.transpose(0, 3, 2, 1),
     )
-    vectors, scales = solve(sizes, diagonals, lmat, forcing)
-    traces, flux = recover(vectors, scales, hmat, forcing)
+    traces, flux = recover(lam, hmat, forcing)
     return (
         traces.reshape(BX, BY, PRESS, BZ, COLS).transpose(0, 1, 3, 2, 4),
         flux.reshape(BX, BY, FLUX, BZ, COLS).transpose(0, 1, 3, 2, 4),

time: 60.4 us -> 49.7 us (0.82)
  local copies, waits for them, and re-layouts: 6.12 us -> 0 us
  Pallas kernels: 53.1 us -> 49 us
    pallas_call x2 -> x1, Pallas kernels: 17.6 us -> 4.43 us  [recover(): pl.pallas_call(recover_kernel, out_shape=out_shape, in_specs=[hbm] * 3, o...]
    pallas_call x1, Pallas kernels: 35.6 us -> 44.5 us  [solve(): pl.pallas_call(functools.partial(solver_kernel, sizes), out_shape=(jax.Sh...]
    unnamed x16 -> x0, local copies, waits for them, and re-layouts: 6.12 us -> none
where the time goes in v3:
time: 49.7 us; the launch traced here: 49.6 us
  Pallas kernels  49 us (99%)
  between operations  0.64 us (1%)
    pallas_call x1, Pallas kernels, solve(): pl.pallas_call(functools.partial(solver_kernel, sizes), out_shape=(jax.Sh...  44.5 us
    pallas_call x1, Pallas kernels, recover(): pl.pallas_call(recover_kernel, out_shape=out_shape, in_specs=[hbm] * 3, o...  4.43 us

profile of v3, /device:TPU:1, one launch (start us, length us, event | category | flops | bytes accessed | tf_op | source)
XLA Modules:
  0.0 49.6 jit_solution(3572247093302683388)
XLA Ops:
  0.6 44.5 %solver.1 = (f32[64,56,128]{2,1,0:T(8,128)}, bf16[64,112,256]{2,1,0:T(8,128)(2,1)}, bf16[64,32,128]{2,1,0:T(8,128)(2,1)}) custom-call(bf16[1728,128]{1,0:T(8,128)(2,1)} %bitcast.12, f32[2,8,4,108]{3,2,1,0:T(4,128)} %refs_1_.1, s32[2,4,8]{2,1,0:T(4,128)} %bitcast.14, f32[3,16]{1,0:T(4,128)} %bitcast.15, f32[108,108]{1,0:T(8,128)} %refs_4_.1, ...), custom_call_target="tpu_custom_call" | custom-call | tf_op jit(solution)/shard_map/solver/pallas_call | solution.py:601
  45.2 4.4 %recover.1 = (f32[1728,128]{1,0:T(8,128)}, bf16[6912,128]{1,0:T(8,128)(2,1)}) custom-call(f32[64,56,128]{2,1,0:T(8,128)} %get-tuple-element.7.lam_hbm, bf16[64,112,256]{2,1,0:T(8,128)(2,1)} %get-tuple-element.8.hmat_hbm, bf16[64,32,128]{2,1,0:T(8,128)(2,1)} %get-tuple-element.9.forcing_hbm), custom_call_target="tpu_custom_call" | custom-call | tf_op jit(solution)/shard_map/recover/pallas_call | solution.py:735

commit v4 on v3

--- a/solution.py
+++ b/solution.py
@@ -32,6 +32,7 @@
 MIB = 1024 * 1024
 
 BATCH = 16
+WIDE = 32
 
 GRANT = 62 * MIB
 
@@ -56,14 +57,9 @@
     return first, jnp.where(kept, second, second - second.astype(BF16).astype(F32)).astype(BF16)
 
 
-def local_blocks(arguments, results, scratch, sems):
+def operand_loads(arguments, scratch, sems):
     sources_hbm, geometry_hbm, rock_hbm, permeability_hbm, mass_hbm, div_hbm, trace_hbm, dirichlet_hbm = arguments
-    diagonals, highs, lows, duals, right = results
-    (
-        geometry, rock, permeability, mass_in, div_map, trace_map, dirichlet, sources,
-        joined, joined_t, padded, scale_t, left_mass, left_joined,
-        press, inverse, table, spread, columns, first, second, solved_in, work,
-    ) = scratch
+    geometry, rock, permeability, mass_in, div_map, trace_map, dirichlet, sources = scratch[:8]
     loads = [
         pltpu.make_async_copy(source, target, sems.at[n])
         for n, (source, target) in enumerate(
@@ -81,6 +77,16 @@
     ]
     for item in loads:
         item.start()
+    return loads
+
+
+def local_blocks(loads, results, scratch):
+    forcing, diagonals, highs, lows, duals, right = results
+    (
+        geometry, rock, permeability, mass_in, div_map, trace_map, dirichlet, sources, lifts,
+        joined, joined_t, padded, scale_t, left_mass, left_joined,
+        press, inverse, table, spread, columns, first, second, solved_in, work,
+    ) = scratch
     joined[...] = jnp.zeros_like(joined)
     padded[...] = jnp.zeros_like(padded)
     inverse[...] = jnp.zeros_like(inverse)
@@ -120,17 +126,17 @@
     scale_t[...] = jnp.transpose(padded[...])
 
     no_rows = jnp.zeros((128 - FR, 256), BF16)
-    for pair in range(BATCH // 2):
+    for pair in range(WIDE // 2):
         for part in range(3):
             first[pair, 128 * part + FR : 128 * part + 128, :] = no_rows
             second[pair, 128 * part + FR : 128 * part + 128, :] = no_rows
 
     on_diagonal = lanes_of((TR, 128)) == rows_of((TR, 128))
 
-    @pl.loop(0, ELEMENTS // BATCH)
+    @pl.loop(0, ELEMENTS // WIDE)
     def build(step):
-        turned = pltpu.roll(scale_t[0:FR, :], lax.rem(128 - BATCH * step, 128), 1)
-        for pair in range(BATCH // 2):
+        turned = pltpu.roll(scale_t[0:FR, :], lax.rem(128 - WIDE * step, 128), 1)
+        for pair in range(WIDE // 2):
             for n in range(2):
                 column = jnp.broadcast_to(turned[:, 2 * pair + n : 2 * pair + n + 1], (FR, 128))
                 cut = slice(128 * n, 128 * n + 128)
@@ -139,22 +145,22 @@
                 first[pair, 0:FR, cut] = high
                 first[pair, 128 : 128 + FR, cut] = low
                 first[pair, 256 : 256 + FR, cut] = high
-        for pair in range(BATCH // 2):
+        for pair in range(WIDE // 2):
             flux_side = columns[pair] * jnp.dot(left_mass[...], first[pair], preferred_element_type=F32)
             high, low = halves(flux_side)
             second[pair, 0:FR, :] = high
             second[pair, 128 : 128 + FR, :] = low
             second[pair, 256 : 256 + FR, :] = high
             for n in range(2):
-                e = step * BATCH + 2 * pair + n
+                e = step * WIDE + 2 * pair + n
                 cut = slice(128 * n, 128 * n + 128)
                 highs[e, TR:AR, :] = high[:, cut]
                 lows[e, TR:AR, :] = low[:, cut]
-        for pair in range(BATCH // 2):
+        for pair in range(WIDE // 2):
             coupled = jnp.dot(left_joined[...], second[pair], preferred_element_type=F32)
             high, low = halves(coupled[0:TR])
             for n in range(2):
-                e = step * BATCH + 2 * pair + n
+                e = step * WIDE + 2 * pair + n
                 cut = slice(128 * n, 128 * n + 128)
                 highs[e, 0:TR, :] = high[:, cut]
                 lows[e, 0:TR, :] = low[:, cut]
@@ -166,21 +172,64 @@
     low_half = lanes_of((PR, 128)) < 64
     row_of = rows_of((PR, 128))
 
-    for pair in range(14):
-        rows = [press[pl.ds(2 * pair + n, ELEMENTS, stride=PR), :] for n in range(2)]
-        work[pair] = jnp.transpose(jnp.concatenate(rows, axis=0))[TR : TR + PR, :]
-
-    for k in range(PRESS):
-        owner, ahead = k // 2, (k + 1) // 2 % 14
-        mine = row_of == k
-        held = low_half if k % 2 == 0 else jnp.logical_not(low_half)
+    early = lanes_of((ELEMENTS, 128)) < TR + PR
+    for quad in range(7):
+        rows = [press[pl.ds(4 * quad + n, ELEMENTS, stride=PR), :] for n in range(4)]
+        stacked = [jnp.where(early, rows[0], rows[2]), jnp.where(early, rows[1], rows[3])]
+        flipped = jnp.transpose(jnp.concatenate(stacked, axis=0))
+        work[2 * quad] = flipped[TR : TR + PR, :]
+        work[2 * quad + 1] = flipped[TR + PR :, :]
+
+    loads[6].wait()
+    loads[7].wait()
+    line = lanes_of((1, 128))
+    x_lanes = (line < 8) | (line == 48)
+    y_lanes = ((line >= 8) & (line < 16)) | (line == 49)
+    z_lanes = ((line >= 16) & (line < 24)) | (line == 50)
+    for part in range(4):
+        spread[part] = sources[432 * part : 432 * part + 432, :].astype(F32)
+
+    def beside(e):
+        i, j, k = e // 32, (e // 4) % 8, e % 4
+        values = spread[e // 16, pl.ds(108 * (j % 4) + k, PRESS, stride=4), :]
+        values = jnp.concatenate([values, jnp.zeros((PR - PRESS, COLS), F32)], axis=0)
+        forcing[e] = values.astype(BF16)
+        lift = [dirichlet[i, normal, k, j].astype(F32) * BLOCKED for normal in range(3)]
+        lifts[e : e + 1, :] = jnp.where(
+            x_lanes, lift[0], jnp.where(y_lanes, lift[1], jnp.where(z_lanes, lift[2], 0.0))
+        )
+
+    for owner in range(13):
+        k = 2 * owner
+        mine, next_one = row_of == k, row_of == k + 1
         source = work[owner]
-        source = jnp.where(held, source, pltpu.roll(source, 64, 1))
-        row = jnp.where(mine, 1.0, source) * (1.0 / source[k : k + 1, :])
-        for pair in [ahead] + [p for p in range(14) if p != ahead]:
+        other = pltpu.roll(source, 64, 1)
+        one, two = jnp.where(low_half, source, other), jnp.where(low_half, other, source)
+        a, b = one[k : k + 1, :], one[k + 1 : k + 2, :]
+        c, d = two[k : k + 1, :], two[k + 1 : k + 2, :]
+        scale = 1.0 / (a * d - b * c)
+        one = jnp.where(mine, 1.0, jnp.where(next_one, 0.0, one))
+        two = jnp.where(mine, 0.0, jnp.where(next_one, 1.0, two))
+        row_one = (d * scale) * one - (b * scale) * two
+        row_two = (a * scale) * two - (c * scale) * one
+        both = mine | next_one
+        for pair in [owner + 1] + [p for p in range(14) if p not in (owner, owner + 1)]:
             value = work[pair]
-            value = jnp.where(mine, 0.0, value) - value[k : k + 1, :] * row
-            work[pair] = jnp.where(held, row, value) if pair == owner else value
+            rest = jnp.where(both, 0.0, value) - value[k : k + 1, :] * row_one
+            work[pair] = rest - value[k + 1 : k + 2, :] * row_two
+        work[owner] = jnp.where(low_half, row_one, row_two)
+        for e in range(5 * owner, min(5 * owner + 5, ELEMENTS)):
+            beside(e)
+
+    k = PRESS - 1
+    mine = row_of == k
+    source = work[13]
+    source = jnp.where(low_half, source, pltpu.roll(source, 64, 1))
+    row = jnp.where(mine, 1.0, source) * (1.0 / source[k : k + 1, :])
+    for pair in range(13):
+        value = work[pair]
+        work[pair] = jnp.where(mine, 0.0, value) - value[k : k + 1, :] * row
+    work[13] = jnp.where(low_half, row, 0.0)
 
     for pair in range(14):
         placed = jnp.concatenate(
@@ -194,27 +243,24 @@
     lane = lanes_of((TR, 256))
     unit = jnp.where((jnp.bitwise_and(lane, 63) == rows_of((TR, 256))) & (lane < 192), 1.0, 0.0)
     unit = unit.astype(BF16)
+    for u in range(WIDE):
+        solved_in[u, PR:TR, :] = jnp.zeros((PR, 128), BF16)
     for u in range(BATCH):
-        solved_in[u, PR:TR, :] = jnp.zeros((PR, 128), BF16)
         right[u, 0:64, :] = unit
         right[u, 128:192, :] = unit
         right[u, 224:256, :] = jnp.zeros((PR, 256), BF16)
     lane = lanes_of((PR, 128))
-    line = lanes_of((1, 128))
-    x_lanes = (line < 8) | (line == 48)
-    y_lanes = ((line >= 8) & (line < 16)) | (line == 49)
-    z_lanes = ((line >= 16) & (line < 24)) | (line == 50)
-
-    @pl.loop(0, ELEMENTS // BATCH)
+
+    @pl.loop(0, ELEMENTS // WIDE)
     def finish(step):
-        for u in range(BATCH):
-            e = step * BATCH + u
+        for u in range(WIDE):
+            e = step * WIDE + u
             high, low = halves(press[pl.ds(pl.multiple_of(e * PR, PR), PR), :])
             solved_in[u, 0:PR, :] = low
             solved_in[u, TR : TR + PR, :] = high
             solved_in[u, TR + PR :, :] = high
-        for u in range(BATCH):
-            e = step * BATCH + u
+        for u in range(WIDE):
+            e = step * WIDE + u
             inv = inverse[pl.ds(pl.multiple_of(e * PR, PR), PR), :]
             left = jnp.where(lane < TR + PR, inv, inv - inv.astype(BF16).astype(F32)).astype(BF16)
             solved = jnp.dot(left, solved_in[u], preferred_element_type=F32)
@@ -226,26 +272,7 @@
                 duals[e, 0:PR, cut] = high
                 duals[e, PR:TR, cut] = low
 
-    loads[6].wait()
-    for e in range(ELEMENTS):
-        i, j, k = e // 32, (e // 4) % 8, e % 4
-        lift = [dirichlet[i, normal, k, j].astype(F32) * BLOCKED for normal in range(3)]
-        diagonals[e : e + 1, :] = diagonals[e : e + 1, :] + jnp.where(
-            x_lanes, lift[0], jnp.where(y_lanes, lift[1], jnp.where(z_lanes, lift[2], 0.0))
-        )
-
-    return loads[7]
-
-
-def spread_forcing(sources, spread, forcing):
-    for part in range(4):
-        spread[...] = sources[432 * part : 432 * part + 432, :].astype(F32)
-        for jj in range(4):
-            for k in range(BZ):
-                e = part * 16 + jj * 4 + k
-                values = spread[pl.ds(108 * jj + k, PRESS, stride=4), :]
-                values = jnp.concatenate([values, jnp.zeros((PR - PRESS, COLS), F32)], axis=0)
-                forcing[e] = values.astype(BF16)
+    diagonals[...] = diagonals[...] + lifts[...]
 
 
 def facet_rows(g, i, jj, k):
@@ -293,6 +320,7 @@
         load_sems, out_sems, send, recv, send_y, recv_y, send_d, recv_d, send_sum, recv_sum,
     ) = refs[11:41]
     local_scratch = refs[41:]
+    loads = operand_loads(arguments, local_scratch, load_sems)
     nx, ny, nz = sizes
     ix, iy, iz = lax.axis_index("gx"), lax.axis_index("gy"), lax.axis_index("gz")
 
@@ -308,9 +336,14 @@
     def at_xy(a, b):
         return (lax.rem(ix + a, nx), lax.rem(iy + b, ny), iz)
 
+    def far(step, count):
+        return -min(step, count - step)
+
+    plane = [(a, b) for a in range(nx) for b in range(ny) if (a, b) != (0, 0)]
+    plane.sort(key=lambda at: far(at[0], nx) + far(at[1], ny))
     rings = [
-        [at_xy(a, b) for a in range(nx) for b in range(ny) if (a, b) != (0, 0)],
-        [at_z(s) for s in range(1, nz)],
+        [at_xy(a, b) for a, b in plane],
+        [at_z(s) for s in sorted(range(1, nz), key=lambda s: far(s, nz))],
     ]
     partners = rings[0] + rings[1]
     barrier = pltpu.get_barrier_semaphore()
@@ -361,9 +394,7 @@
             return field_copy(low, stage, first, last, GROUP, send_y.at[stage, 0], recv_y.at[stage, 0], at_y(-1))
         return field_copy(up, stage, last, first, GROUP, send_y.at[stage, 1], recv_y.at[stage, 1], at_y(1))
 
-    sources_load = local_blocks(
-        arguments, (diagonals, highs, lows, duals, right), local_scratch, load_sems
-    )
+    local_blocks(loads, (forcing, diagonals, highs, lows, duals, right), local_scratch)
     pl.semaphore_wait(barrier, len(partners))
 
     half = ELEMENTS // 2
@@ -389,8 +420,6 @@
             def _():
                 copy_y(stage, side).start()
 
-    sources_load.wait()
-    spread_forcing(local_scratch[7], local_scratch[17], forcing)
     out_copies = [pltpu.make_async_copy(forcing, forcing_hbm, out_sems.at[0])]
     out_copies[0].start()
 
@@ -534,6 +563,17 @@
             hmat[e, :, 0:128] = both.astype(BF16)
             hmat[e, :, 128:256] = rest
 
+    def drain():
+        @pl.loop(0, 4)
+        def _(g):
+            for stage in range(3):
+                for item in copies_xz(stage, g):
+                    item.wait_send()
+
+        for stage in range(3):
+            for side in range(2):
+                copy_y(stage, side).wait_send()
+
     batches = ELEMENTS // BATCH
     for stage, (ring, parts) in enumerate(zip(rings, (parts_a, parts_b))):
         mine[stage] = tile
@@ -544,6 +584,8 @@
         place = pl.ds(span[0] * BATCH, (span[1] - span[0]) * BATCH)
         out_copies.append(pltpu.make_async_copy(hmat.at[place], hmat_hbm.at[place], out_sems.at[1 + stage]))
         out_copies[-1].start()
+        if stage == 1:
+            drain()
         pltpu.make_async_copy(parts, parts, recv_sum.at[stage]).wait()
         terms = [tile] + [parts[n] for n in range(len(ring))]
         while len(terms) > 1:
@@ -567,28 +609,19 @@
     c0, c1, c2 = [jnp.broadcast_to(c, (8, COLS)) for c in (c0, c1, c2)]
 
     for part in range(2):
-        @pl.loop(32 * part, 32 * part + 32)
-        def combine(e):
-            for tile in range(7):
-                place = slice(8 * tile, 8 * tile + 8)
-                lam[e, place, :] = (
-                    c0 * vectors[0, e, place, :] + c1 * vectors[1, e, place, :] + c2 * vectors[2, e, place, :]
-                )
+        @pl.loop(8 * part, 8 * part + 8)
+        def combine(step):
+            for u in range(4):
+                e = 4 * step + u
+                for tile in range(7):
+                    place = slice(8 * tile, 8 * tile + 8)
+                    lam[e, place, :] = (
+                        c0 * vectors[0, e, place, :] + c1 * vectors[1, e, place, :] + c2 * vectors[2, e, place, :]
+                    )
 
         place = pl.ds(32 * part, 32)
         out_copies.append(pltpu.make_async_copy(lam.at[place], lam_hbm.at[place], out_sems.at[3 + part]))
         out_copies[-1].start()
-
-    @pl.loop(0, 4)
-    def drain(g):
-        for stage in range(3):
-            for item in copies_xz(stage, g):
-                item.wait_send()
-
-    for stage in range(3):
-        for side in range(2):
-            copy_y(stage, side).wait_send()
-
 
     for item in out_copies:
         item.wait()
@@ -638,6 +671,7 @@
             pltpu.VMEM(trace_map.shape, F32),
             pltpu.SMEM(dirichlet.shape, jnp.int32),
             pltpu.VMEM((ELEMENTS * PRESS, COLS), BF16),
+            pltpu.VMEM((ELEMENTS, 128), F32),
             pltpu.VMEM((128, 128), F32),
             pltpu.VMEM((128, 128), F32),
             pltpu.VMEM((128, 128), F32),
@@ -647,11 +681,11 @@
             pltpu.VMEM((ELEMENTS * PR, 128), F32),
             pltpu.VMEM((ELEMENTS * PR, 128), F32),
             pltpu.VMEM((16, 128), F32),
-            pltpu.VMEM((432, 128), F32),
-            pltpu.VMEM((BATCH // 2, FR, 256), F32),
-            pltpu.VMEM((BATCH // 2, 384, 256), BF16),
-            pltpu.VMEM((BATCH // 2, 384, 256), BF16),
-            pltpu.VMEM((BATCH, 128, 128), BF16),
+            pltpu.VMEM((4, 432, 128), F32),
+            pltpu.VMEM((WIDE // 2, FR, 256), F32),
+            pltpu.VMEM((WIDE // 2, 384, 256), BF16),
+            pltpu.VMEM((WIDE // 2, 384, 256), BF16),
+            pltpu.VMEM((WIDE, 128, 128), BF16),
             pltpu.VMEM((14, PR, 128), F32),
         ],
         compiler_params=pltpu.CompilerParams(

time: 49.7 us -> 47.1 us (0.948)
  Pallas kernels: 49 us -> 46.4 us
    pallas_call x1, Pallas kernels: 44.5 us -> 42 us  [solve(): pl.pallas_call(functools.partial(solver_kernel, sizes), out_shape=(jax.Sh...]
where the time goes in v4:
time: 47.1 us; the launch traced here: 47 us
  Pallas kernels  46.4 us (99%)
  between operations  0.64 us (1%)
    pallas_call x1, Pallas kernels, solve(): pl.pallas_call(functools.partial(solver_kernel, sizes), out_shape=(jax.Sh...  42 us
    pallas_call x1, Pallas kernels, recover(): pl.pallas_call(recover_kernel, out_shape=out_shape, in_specs=[hbm] * 3, o...  4.42 us

profile of v4, /device:TPU:1, one launch (start us, length us, event | category | flops | bytes accessed | tf_op | source)
XLA Modules:
  0.0 47.0 jit_solution(11524779046661355761)
XLA Ops:
  0.6 42.0 %solver.1 = (f32[64,56,128]{2,1,0:T(8,128)}, bf16[64,112,256]{2,1,0:T(8,128)(2,1)}, bf16[64,32,128]{2,1,0:T(8,128)(2,1)}) custom-call(bf16[1728,128]{1,0:T(8,128)(2,1)} %bitcast.12, f32[2,8,4,108]{3,2,1,0:T(4,128)} %refs_1_.1, s32[2,4,8]{2,1,0:T(4,128)} %bitcast.14, f32[3,16]{1,0:T(4,128)} %bitcast.15, f32[108,108]{1,0:T(8,128)} %refs_4_.1, ...), custom_call_target="tpu_custom_call" | custom-call | tf_op jit(solution)/shard_map/solver/pallas_call | solution.py:634
  42.6 4.4 %recover.1 = (f32[1728,128]{1,0:T(8,128)}, bf16[6912,128]{1,0:T(8,128)(2,1)}) custom-call(f32[64,56,128]{2,1,0:T(8,128)} %get-tuple-element.7.lam_hbm, bf16[64,112,256]{2,1,0:T(8,128)(2,1)} %get-tuple-element.8.hmat_hbm, bf16[64,32,128]{2,1,0:T(8,128)(2,1)} %get-tuple-element.9.forcing_hbm), custom_call_target="tpu_custom_call" | custom-call | tf_op jit(solution)/shard_map/recover/pallas_call | solution.py:769

commit v5 on v4

--- a/solution.py
+++ b/solution.py
@@ -275,15 +275,23 @@
     diagonals[...] = diagonals[...] + lifts[...]
 
 
+def j_of(g, jj):
+    return (2 * g + 7 + jj) % 8 if isinstance(g, int) else lax.rem(2 * g + 7 + jj, 8)
+
+
+def row_hint(row):
+    return row if isinstance(row, int) else pl.multiple_of(row, 8)
+
+
 def facet_rows(g, i, jj, k):
     places = []
     for side in range(2):
         for start, size, slot in (
             (((i + side) * 4 + g) * GROUP, 64, jj * 4 + k),
-            (Y_START + (2 * g + jj + side) * GROUP, 64, i * 4 + k),
+            (Y_START + (j_of(g, jj) + side) * GROUP, 64, i * 4 + k),
             (Z_START + ((k + side) * 4 + g) * Z_GROUP, 32, i * 2 + jj),
         ):
-            places.append((pl.multiple_of(start + slot * 8, 8), start + size + slot))
+            places.append((row_hint(start + slot * 8), start + size + slot))
     return places
 
 
@@ -309,7 +317,7 @@
 
 
 def element_index(g, i, jj, k):
-    return i * 32 + g * 8 + jj * 4 + k
+    return i * 32 + j_of(g, jj) * 4 + k
 
 
 def solver_kernel(sizes, *refs):
@@ -373,8 +381,8 @@
 
     def field_copy(buffer, stage, source, target, count, sent, received, device):
         return remote(
-            buffer.at[stage, pl.ds(pl.multiple_of(source, 8), count)],
-            buffer.at[stage, pl.ds(pl.multiple_of(target, 8), count)],
+            buffer.at[stage, pl.ds(row_hint(source), count)],
+            buffer.at[stage, pl.ds(row_hint(target), count)],
             sent, received, device,
         )
 
@@ -409,16 +417,19 @@
     for item in near_copies:
         item.start()
 
-    def order(n):
-        return lax.rem(3 * n, 4)
-
-    def send_chunk(stage, n):
-        for item in copies_xz(stage, order(n)):
+    def send_chunk(stage, g):
+        for item in copies_xz(stage, g):
             item.start()
-        for side in range(2):
-            @pl.when(n == side)
-            def _():
+
+        def both_y():
+            for side in range(2):
                 copy_y(stage, side).start()
+
+        if isinstance(g, int):
+            if g == 0:
+                both_y()
+        else:
+            pl.when(g == 0)(both_y)
 
     out_copies = [pltpu.make_async_copy(forcing, forcing_hbm, out_sems.at[0])]
     out_copies[0].start()
@@ -429,8 +440,7 @@
         right[u, 192:224, :] = duals[e, 0:PR, :]
 
     @pl.loop(0, 4)
-    def start(n):
-        g = order(n)
+    def start(g):
         for u, (i, jj, k) in enumerate(EACH):
             fill_right(u, element_index(g, i, jj, k))
         for u, (i, jj, k) in enumerate(EACH):
@@ -444,7 +454,7 @@
             given = jnp.concatenate([jnp.zeros((TR, COLS), BF16), forcing[e], forcing[e]], axis=0)
             values = -jnp.dot(lmat[e, :, 128:256], given, preferred_element_type=F32)
             scatter(values, low.at[0], up.at[0], facet_rows(g, i, jj, k))
-        send_chunk(0, n)
+        send_chunk(0, g)
 
     for item in near_copies:
         item.wait()
@@ -472,14 +482,13 @@
     turned[0:24, :] = flipped[0:24]
     turned[24:32, :] = flipped[48:56]
 
-    @pl.loop(0, 4)
-    def expand(g):
-        rolled = pltpu.roll(turned[...], lax.rem(128 - 8 * g, 128), 1)
+    rolled = turned[...]
+    for g in range(4):
         for i, jj, k in EACH:
-            column = i * 32 + jj * 4 + k
+            column = element_index(g, i, jj, k)
             places = facet_rows(g, i, jj, k)
             for side in range(2):
-                normals = [0, 1, 2] if side == 0 else [n for n, last in enumerate((i == 1, jj == 1, k == 3)) if last]
+                normals = [0, 1, 2] if side == 0 else [n for n, last in enumerate((i == 1, j_of(g, jj) == 7, k == 3)) if last]
                 if not normals:
                     continue
                 at = 64 * side + column
@@ -493,11 +502,13 @@
 
     def update(step, g, total):
         spans = [((plane * 4 + g) * GROUP, 9, plane < 2) for plane in range(3)]
-        spans += [(Y_START + (2 * g + plane) * GROUP, 9, plane < 2) for plane in range(3)]
+        lowers = [j_of(g, jj) for jj in range(2)]
+        spans += [(Y_START + plane * GROUP, 9, True) for plane in lowers]
+        spans += [(Y_START + (j + 1) * GROUP, 9, False) for j in lowers if j + 1 not in lowers]
         spans += [(Z_START + (plane * 4 + g) * Z_GROUP, 5, plane < 4) for plane in range(5)]
         for begin, tiles, owned in spans:
             for tile in range(tiles):
-                place = pl.ds(pl.multiple_of(begin + tile * 8, 8), 8)
+                place = pl.ds(begin + tile * 8, 8)
                 value = low[step, place, :] + up[step, place, :]
                 scaled = inverse[place, :] * value
                 if step == 0:
@@ -508,14 +519,11 @@
                     fields[step, place, :] = scaled - fields[step - 1, place, :]
         return total
 
-    def operate(step, n, totals):
-        g = order(n)
-        totals = list(totals)
+    def operate(step, g, totals):
         for item in copies_xz(step, g):
             item.wait_recv()
-        for side in range(2):
-            @pl.when(n == 1 - side)
-            def _():
+        if g == 0:
+            for side in range(2):
                 copy_y(step, side).wait_recv()
         totals[0] = update(step, g, totals[0])
         for u, (i, jj, k) in enumerate(EACH):
@@ -538,12 +546,13 @@
             if step < 2:
                 scatter(values, low.at[step + 1], up.at[step + 1], facet_rows(g, i, jj, k))
         if step < 2:
-            send_chunk(step + 1, n)
-        return tuple(totals)
+            send_chunk(step + 1, g)
 
     moments = []
     for step in range(3):
-        totals = lax.fori_loop(0, 4, functools.partial(operate, step), (zero,) * 3)
+        totals = [zero] * 3
+        for g in range(4):
+            operate(step, g, totals)
         moments += [totals[:2], totals[1:], totals[1:]][step]
 
     sublane = rows_of((8, COLS))

time: 47.1 us -> 46.2 us (0.981)
  Pallas kernels: 46.4 us -> 45.4 us
    pallas_call x1, Pallas kernels: 42 us -> 41 us  [solve(): pl.pallas_call(functools.partial(solver_kernel, sizes), out_shape=(jax.Sh...]
where the time goes in v5:
time: 46.2 us; the launch traced here: 46.1 us
  Pallas kernels  45.4 us (98%)
  between operations  0.64 us (1%)
    pallas_call x1, Pallas kernels, solve(): pl.pallas_call(functools.partial(solver_kernel, sizes), out_shape=(jax.Sh...  41 us
    pallas_call x1, Pallas kernels, recover(): pl.pallas_call(recover_kernel, out_shape=out_shape, in_specs=[hbm] * 3, o...  4.43 us

profile of v5, /device:TPU:1, one launch (start us, length us, event | category | flops | bytes accessed | tf_op | source)
XLA Modules:
  0.0 46.1 jit_solution(1796672796099962668)
XLA Ops:
  0.6 41.0 %solver.1 = (f32[64,56,128]{2,1,0:T(8,128)}, bf16[64,112,256]{2,1,0:T(8,128)(2,1)}, bf16[64,32,128]{2,1,0:T(8,128)(2,1)}) custom-call(bf16[1728,128]{1,0:T(8,128)(2,1)} %bitcast.12, f32[2,8,4,108]{3,2,1,0:T(4,128)} %refs_1_.1, s32[2,4,8]{2,1,0:T(4,128)} %bitcast.14, f32[3,16]{1,0:T(4,128)} %bitcast.15, f32[108,108]{1,0:T(8,128)} %refs_4_.1, ...), custom_call_target="tpu_custom_call" | custom-call | tf_op jit(solution)/shard_map/solver/pallas_call | solution.py:643
  41.6 4.4 %recover.1 = (f32[1728,128]{1,0:T(8,128)}, bf16[6912,128]{1,0:T(8,128)(2,1)}) custom-call(f32[64,56,128]{2,1,0:T(8,128)} %get-tuple-element.7.lam_hbm, bf16[64,112,256]{2,1,0:T(8,128)(2,1)} %get-tuple-element.8.hmat_hbm, bf16[64,32,128]{2,1,0:T(8,128)(2,1)} %get-tuple-element.9.forcing_hbm), custom_call_target="tpu_custom_call" | custom-call | tf_op jit(solution)/shard_map/recover/pallas_call | solution.py:778

commit v6 on v5

--- a/solution.py
+++ b/solution.py
@@ -421,15 +421,9 @@
         for item in copies_xz(stage, g):
             item.start()
 
-        def both_y():
+        if g == 0:
             for side in range(2):
                 copy_y(stage, side).start()
-
-        if isinstance(g, int):
-            if g == 0:
-                both_y()
-        else:
-            pl.when(g == 0)(both_y)
 
     out_copies = [pltpu.make_async_copy(forcing, forcing_hbm, out_sems.at[0])]
     out_copies[0].start()
@@ -439,7 +433,6 @@
         right[u, 96:128, :] = duals[e, PR:TR, :]
         right[u, 192:224, :] = duals[e, 0:PR, :]
 
-    @pl.loop(0, 4)
     def start(g):
         for u, (i, jj, k) in enumerate(EACH):
             fill_right(u, element_index(g, i, jj, k))
@@ -455,6 +448,9 @@
             values = -jnp.dot(lmat[e, :, 128:256], given, preferred_element_type=F32)
             scatter(values, low.at[0], up.at[0], facet_rows(g, i, jj, k))
         send_chunk(0, g)
+
+    for g in range(4):
+        start(g)
 
     for item in near_copies:
         item.wait()

time: 46.2 us -> 46.1 us (level)
  no operation moved by 1% of the time
where the time goes in v6:
time: 46.1 us; the launch traced here: 46 us
  Pallas kernels  45.3 us (98%)
  between operations  0.64 us (1%)
    pallas_call x1, Pallas kernels, solve(): pl.pallas_call(functools.partial(solver_kernel, sizes), out_shape=(jax.Sh...  40.9 us
    pallas_call x1, Pallas kernels, recover(): pl.pallas_call(recover_kernel, out_shape=out_shape, in_specs=[hbm] * 3, o...  4.42 us

profile of v6, /device:TPU:1, one launch (start us, length us, event | category | flops | bytes accessed | tf_op | source)
XLA Modules:
  0.0 46.0 jit_solution(1732788941853635821)
XLA Ops:
  0.6 40.9 %solver.1 = (f32[64,56,128]{2,1,0:T(8,128)}, bf16[64,112,256]{2,1,0:T(8,128)(2,1)}, bf16[64,32,128]{2,1,0:T(8,128)(2,1)}) custom-call(bf16[1728,128]{1,0:T(8,128)(2,1)} %bitcast.12, f32[2,8,4,108]{3,2,1,0:T(4,128)} %refs_1_.1, s32[2,4,8]{2,1,0:T(4,128)} %bitcast.14, f32[3,16]{1,0:T(4,128)} %bitcast.15, f32[108,108]{1,0:T(8,128)} %refs_4_.1, ...), custom_call_target="tpu_custom_call" | custom-call | tf_op jit(solution)/shard_map/solver/pallas_call | solution.py:639
  41.5 4.4 %recover.1 = (f32[1728,128]{1,0:T(8,128)}, bf16[6912,128]{1,0:T(8,128)(2,1)}) custom-call(f32[64,56,128]{2,1,0:T(8,128)} %get-tuple-element.7.lam_hbm, bf16[64,112,256]{2,1,0:T(8,128)(2,1)} %get-tuple-element.8.hmat_hbm, bf16[64,32,128]{2,1,0:T(8,128)(2,1)} %get-tuple-element.9.forcing_hbm), custom_call_target="tpu_custom_call" | custom-call | tf_op jit(solution)/shard_map/recover/pallas_call | solution.py:774
